TPU v7x, 32 devices: a whole 2x2x4 slice. The times are simulated.
32 devices in a mesh: dp: 4 (over y, x), fsdp: 8 (over z, core).
Axes of the slice: x: 2, y: 2, z: 4, core: 2. Of those that a mesh axis runs over, the one named last changes fastest.
Arguments:
- tokens: bfloat16 [8, 1024, 1536], P('fsdp', 'dp'), may hold values from -13 to 13
- cotangent: bfloat16 [4, 8, 1024, 1536], P(None, 'fsdp', 'dp'), may hold values from -6 to 6
- norm1_gain: bfloat16 [1536], P(('dp', 'fsdp')), may hold values from 0.25 to 1.75
- norm1_bias: bfloat16 [1536], P(('dp', 'fsdp')), may hold values from -3 to 3
- query_weight: bfloat16 [1536, 1536], P(('dp', 'fsdp')), may hold values from -0.15625 to 0.15625
- key_weight: bfloat16 [1536, 1536], P(('dp', 'fsdp')), may hold values from -0.15625 to 0.15625
- value_weight: bfloat16 [1536, 1536], P(('dp', 'fsdp')), may hold values from -0.15625 to 0.15625
- out_weight: bfloat16 [1536, 1536], P(('dp', 'fsdp')), may hold values from -3.5 to 3.5
- norm2_gain: bfloat16 [1536], P(('dp', 'fsdp')), may hold values from 0.25 to 1.75
- norm2_bias: bfloat16 [1536], P(('dp', 'fsdp')), may hold values from -3 to 3
- up_weight: bfloat16 [1536, 6144], P(('dp', 'fsdp')), may hold values from -0.15625 to 0.15625
- up_bias: bfloat16 [6144], P(('dp', 'fsdp')), may hold values from -3 to 3
- down_weight: bfloat16 [6144, 1536], P(('dp', 'fsdp')), may hold values from -0.15625 to 0.15625
- down_bias: bfloat16 [1536], P(('dp', 'fsdp')), may hold values from -3 to 3
Outputs:
- activations: bfloat16 [4, 8, 1024, 1536], P(None, 'fsdp', 'dp')
- grad_tokens: bfloat16 [8, 1024, 1536], P('fsdp', 'dp')
- grad_norm1_gain: float32 [1536], P(('dp', 'fsdp'))
- grad_norm1_bias: float32 [1536], P(('dp', 'fsdp'))
- grad_query_weight: float32 [1536, 1536], P(('dp', 'fsdp'))
- grad_key_weight: float32 [1536, 1536], P(('dp', 'fsdp'))
- grad_value_weight: float32 [1536, 1536], P(('dp', 'fsdp'))
- grad_out_weight: float32 [1536, 1536], P(('dp', 'fsdp'))
- grad_norm2_gain: float32 [1536], P(('dp', 'fsdp'))
- grad_norm2_bias: float32 [1536], P(('dp', 'fsdp'))
- grad_up_weight: float32 [1536, 6144], P(('dp', 'fsdp'))
- grad_up_bias: float32 [6144], P(('dp', 'fsdp'))
- grad_down_weight: float32 [6144, 1536], P(('dp', 'fsdp'))
- grad_down_bias: float32 [1536], P(('dp', 'fsdp'))
All inputs are finite; a program needn't handle non-finite values.
Results may differ from a plain program's by a relative error of at most 0.019.
Values may be sent and summed in bfloat16 or wider, within the bound.
A program may use at most 320 MiB of HBM per device.

v0:
```python
import math

import jax
import jax.numpy as jnp
from jax import lax
from jax.sharding import PartitionSpec as P

HEADS = 12
HEAD_DIM = 128
FF = 6144
GRAN = 4


epsilon = 1e-05
masked_score = -1e30


def product(left, right):
    return jnp.dot(left, right, preferred_element_type=jnp.float32)


def gram_product(left, right):
    return lax.dot_general(
        left, right, (((0,), (0,)), ((), ())), preferred_element_type=jnp.float32
    )


def back_product(left, right):
    return lax.dot_general(
        left, right, (((1,), (1,)), ((), ())), preferred_element_type=jnp.float32
    )


def norm_parts(values):
    centred = values - jnp.mean(values, axis=-1, keepdims=True)
    inverse = lax.rsqrt(jnp.mean(centred * centred, axis=-1, keepdims=True) + epsilon)
    return (centred * inverse, inverse)


def norm_backward(grad_normed, normed, inverse, gain):
    scaled = grad_normed * gain
    return inverse * (
        scaled
        - jnp.mean(scaled, axis=-1, keepdims=True)
        - normed * jnp.mean(scaled * normed, axis=-1, keepdims=True)
    )


def gelu_value(values):
    return (
        0.5
        * values
        * (1.0 + jnp.tanh(0.7978845608028654 * (values + 0.044715 * values * values * values)))
    )


def gelu_grad(values):
    tangent = jnp.tanh(0.7978845608028654 * (values + 0.044715 * values * values * values))
    return 0.5 * (1.0 + tangent) + 0.5 * values * (1.0 - tangent * tangent) * 0.7978845608028654 * (
        1.0 + 3.0 * 0.044715 * values * values
    )


def rotary_tables(positions, half_size):
    ladder = jnp.arange(half_size).astype(jnp.float32)
    inverse = jnp.exp(ladder * (-math.log(10000.0) / half_size))
    angles = positions[:, None] * inverse[None, :]
    return (jnp.cos(angles)[:, None, :], jnp.sin(angles)[:, None, :])


def rotate(values, cosine, sine):
    half_size = values.shape[-1] // 2
    first = values[..., :half_size]
    second = values[..., half_size:]
    return jnp.concatenate(
        [first * cosine - second * sine, second * cosine + first * sine], axis=-1
    )


def block_scores(queries, positions, key_block, start_row):
    block_rows = key_block.shape[0]
    scores = jnp.einsum("qhd,khd->hqk", queries, key_block, preferred_element_type=jnp.float32)
    key_positions = start_row + jnp.arange(block_rows, dtype=jnp.int32)
    visible = positions[None, :, None] >= key_positions[None, None, :]
    return (jnp.where(visible, scores, masked_score), visible)


def key_blocking(keys_all, values_all, key_offset):
    seq_len = keys_all.shape[0]
    block_rows = min(512, seq_len)
    block_count = seq_len // block_rows
    key_blocks = keys_all.reshape(block_count, block_rows, HEADS, HEAD_DIM)
    value_blocks = values_all.reshape(block_count, block_rows, HEADS, HEAD_DIM)
    starts = key_offset + jnp.arange(block_count, dtype=jnp.int32) * block_rows
    return (key_blocks, value_blocks, starts)


def attend(queries, keys_all, values_all, positions):
    tok_rows = queries.shape[0]
    key_blocks, value_blocks, starts = key_blocking(keys_all, values_all, jnp.int32(0))

    def measure(state_pair, block_pair):
        top_score, total = state_pair
        key_block, start_row = block_pair
        scores, visible = block_scores(queries, positions, key_block, start_row)
        new_top = jnp.maximum(top_score, jnp.max(scores, axis=-1))
        raised = jnp.where(visible, jnp.exp(scores - new_top[..., None]), 0.0)
        total = total * jnp.exp(top_score - new_top) + jnp.sum(raised, axis=-1)
        return ((new_top, total), None)

    initial = (
        jnp.full((HEADS, tok_rows), masked_score, jnp.float32),
        jnp.zeros((HEADS, tok_rows), jnp.float32),
    )
    (top_score, total), unused = lax.scan(measure, initial, (key_blocks, starts))
    log_total = top_score + jnp.log(total)

    def accumulate(mixed, block_triple):
        key_block, value_block, start_row = block_triple
        scores, visible = block_scores(queries, positions, key_block, start_row)
        probs = jnp.where(visible, jnp.exp(scores - log_total[..., None]), 0.0).astype(jnp.bfloat16)
        return (
            mixed
            + jnp.einsum("hqk,khd->qhd", probs, value_block, preferred_element_type=jnp.float32),
            None,
        )

    mixed, unused = lax.scan(
        accumulate,
        jnp.zeros((tok_rows, HEADS, HEAD_DIM), jnp.float32),
        (key_blocks, value_blocks, starts),
    )
    return (mixed, log_total)


def attend_back(
    queries, positions, keys_all, values_all, key_offset, grad_mixed, log_total, row_delta
):
    tok_rows = queries.shape[0]
    key_blocks, value_blocks, starts = key_blocking(keys_all, values_all, key_offset)

    def backward_block(grad_queries, block_triple):
        key_block, value_block, start_row = block_triple
        scores, visible = block_scores(queries, positions, key_block, start_row)
        probs = jnp.where(visible, jnp.exp(scores - log_total[..., None]), 0.0)
        grad_probs = jnp.einsum(
            "qhd,khd->hqk", grad_mixed, value_block, preferred_element_type=jnp.float32
        )
        grad_scores = (probs * (grad_probs - row_delta[..., None])).astype(jnp.bfloat16)
        grad_queries = grad_queries + jnp.einsum(
            "hqk,khd->qhd", grad_scores, key_block, preferred_element_type=jnp.float32
        )
        grad_key_block = jnp.einsum(
            "hqk,qhd->khd", grad_scores, queries, preferred_element_type=jnp.float32
        )
        grad_value_block = jnp.einsum(
            "hqk,qhd->khd",
            probs.astype(jnp.bfloat16),
            grad_mixed,
            preferred_element_type=jnp.float32,
        )
        return (grad_queries, (grad_key_block, grad_value_block))

    grad_queries, (grad_keys, grad_values) = lax.scan(
        backward_block,
        jnp.zeros((tok_rows, HEADS, HEAD_DIM), jnp.float32),
        (key_blocks, value_blocks, starts),
    )
    key_len = keys_all.shape[0]
    return (
        grad_queries,
        grad_keys.reshape(key_len, HEADS * HEAD_DIM),
        grad_values.reshape(key_len, HEADS * HEAD_DIM),
    )


def local(
    tokens,
    cotangent,
    norm1_gain,
    norm1_bias,
    query_weight,
    key_weight,
    value_weight,
    out_weight,
    norm2_gain,
    norm2_bias,
    up_weight,
    up_bias,
    down_weight,
    down_bias,
):
    (
        gain_one,
        bias_one,
        w_query,
        w_key,
        w_value,
        w_out,
        gain_two,
        bias_two,
        w_up,
        b_up,
        w_down,
        b_down,
    ) = (
        lax.all_gather(norm1_gain, ("dp", "fsdp"), axis=0, tiled=True),
        lax.all_gather(norm1_bias, ("dp", "fsdp"), axis=0, tiled=True),
        lax.all_gather(query_weight, ("dp", "fsdp"), axis=0, tiled=True),
        lax.all_gather(key_weight, ("dp", "fsdp"), axis=0, tiled=True),
        lax.all_gather(value_weight, ("dp", "fsdp"), axis=0, tiled=True),
        lax.all_gather(out_weight, ("dp", "fsdp"), axis=0, tiled=True),
        lax.all_gather(norm2_gain, ("dp", "fsdp"), axis=0, tiled=True),
        lax.all_gather(norm2_bias, ("dp", "fsdp"), axis=0, tiled=True),
        lax.all_gather(up_weight, ("dp", "fsdp"), axis=0, tiled=True),
        lax.all_gather(up_bias, ("dp", "fsdp"), axis=0, tiled=True),
        lax.all_gather(down_weight, ("dp", "fsdp"), axis=0, tiled=True),
        lax.all_gather(down_bias, ("dp", "fsdp"), axis=0, tiled=True),
    )
    seq_count = tokens.shape[0]
    tok_rows = tokens.shape[1]
    model_width = tokens.shape[2]
    all_rows = seq_count * tok_rows
    scaling = HEAD_DIM ** (-0.5)
    inputs = tokens.reshape(all_rows, model_width).astype(jnp.float32)
    normed_one, inverse_one = norm_parts(inputs)
    attn_in = (normed_one * gain_one.astype(jnp.float32) + bias_one.astype(jnp.float32)).astype(
        jnp.bfloat16
    )
    queries = product(attn_in, w_query).reshape(seq_count, tok_rows, HEADS, HEAD_DIM)
    key_raw = product(attn_in, w_key).reshape(seq_count, tok_rows, HEADS, HEAD_DIM)
    value_low = (
        product(attn_in, w_value).astype(jnp.bfloat16).reshape(seq_count, tok_rows, model_width)
    )
    key_offset = lax.axis_index("dp") * tok_rows
    positions = key_offset + jnp.arange(tok_rows, dtype=jnp.int32)
    cosine, sine = rotary_tables(positions.astype(jnp.float32), HEAD_DIM // 2)
    q_rot = (rotate(queries, cosine, sine) * scaling).astype(jnp.bfloat16)
    k_flat = (
        rotate(key_raw, cosine, sine).astype(jnp.bfloat16).reshape(seq_count, tok_rows, model_width)
    )
    keys_all, values_all = (
        lax.all_gather(k_flat, "dp", axis=1, tiled=True),
        lax.all_gather(value_low, "dp", axis=1, tiled=True),
    )
    seq_len = keys_all.shape[1]
    mixed, log_total = jax.vmap(attend, in_axes=(0, 0, 0, None))(
        q_rot,
        keys_all.reshape(seq_count, seq_len, HEADS, HEAD_DIM),
        values_all.reshape(seq_count, seq_len, HEADS, HEAD_DIM),
        positions,
    )
    mixed_low = mixed.reshape(all_rows, model_width).astype(jnp.bfloat16)
    hidden = inputs + product(mixed_low, w_out)
    normed_two, inverse_two = norm_parts(hidden)
    ffn_in = (normed_two * gain_two.astype(jnp.float32) + bias_two.astype(jnp.float32)).astype(
        jnp.bfloat16
    )
    preact = product(ffn_in, w_up) + b_up.astype(jnp.float32)
    edges = [0] + [FF // 2 ** (GRAN - 1 - level_idx) for level_idx in range(GRAN)]
    gated_list = []
    result_list = []
    for level_idx in range(GRAN):
        level_width = edges[level_idx + 1]
        gated = gelu_value(preact[:, :level_width]).astype(jnp.bfloat16)
        gated_list.append(gated)
        result = hidden + product(gated, w_down[:level_width]) + b_down.astype(jnp.float32)
        result_list.append(result.astype(jnp.bfloat16))
    activations = jnp.stack(result_list).reshape(GRAN, seq_count, tok_rows, model_width)
    back_gain_one, back_query, back_key, back_value, back_out, back_gain_two, back_up, back_down = (
        lax.all_gather(norm1_gain, ("dp", "fsdp"), axis=0, tiled=True),
        lax.all_gather(query_weight, ("dp", "fsdp"), axis=0, tiled=True),
        lax.all_gather(key_weight, ("dp", "fsdp"), axis=0, tiled=True),
        lax.all_gather(value_weight, ("dp", "fsdp"), axis=0, tiled=True),
        lax.all_gather(out_weight, ("dp", "fsdp"), axis=0, tiled=True),
        lax.all_gather(norm2_gain, ("dp", "fsdp"), axis=0, tiled=True),
        lax.all_gather(up_weight, ("dp", "fsdp"), axis=0, tiled=True),
        lax.all_gather(down_weight, ("dp", "fsdp"), axis=0, tiled=True),
    )
    grads_out = cotangent.reshape(GRAN, all_rows, model_width)
    grad_hidden = jnp.sum(grads_out.astype(jnp.float32), axis=0)
    grad_down_bias = jnp.sum(grad_hidden, axis=0)
    grad_ffn_in = jnp.zeros((all_rows, model_width), jnp.float32)
    pre_grads = []
    for level_idx in range(GRAN):
        level_width = edges[level_idx + 1]
        grad_gated = back_product(grads_out[level_idx], back_down[:level_width])
        grad_pre = (grad_gated * gelu_grad(preact[:, :level_width])).astype(jnp.bfloat16)
        pre_grads.append(grad_pre)
        grad_ffn_in = grad_ffn_in + back_product(grad_pre, back_up[:, :level_width])
    up_blocks = []
    bias_blocks = []
    down_blocks = []
    for block_idx in range(GRAN):
        start_col = edges[block_idx]
        stop_col = edges[block_idx + 1]
        stacked_grad = jnp.concatenate(
            [pre_grads[level_idx][:, start_col:stop_col] for level_idx in range(block_idx, GRAN)],
            axis=0,
        )
        stacked_in = jnp.concatenate([ffn_in] * (GRAN - block_idx), axis=0)
        up_blocks.append(gram_product(stacked_in, stacked_grad))
        bias_blocks.append(jnp.sum(stacked_grad.astype(jnp.float32), axis=0))
        stacked_gated = jnp.concatenate(
            [gated_list[level_idx][:, start_col:stop_col] for level_idx in range(block_idx, GRAN)],
            axis=0,
        )
        stacked_out = jnp.concatenate(
            [grads_out[level_idx] for level_idx in range(block_idx, GRAN)], axis=0
        )
        down_blocks.append(gram_product(stacked_gated, stacked_out))
    grad_up_weight = jnp.concatenate(up_blocks, axis=1)
    grad_up_bias = jnp.concatenate(bias_blocks, axis=0)
    grad_down_weight = jnp.concatenate(down_blocks, axis=0)
    grad_gain_two = jnp.sum(grad_ffn_in * normed_two, axis=0)
    grad_bias_two = jnp.sum(grad_ffn_in, axis=0)
    grad_hidden = grad_hidden + norm_backward(
        grad_ffn_in, normed_two, inverse_two, back_gain_two.astype(jnp.float32)
    )
    grad_branch = grad_hidden.astype(jnp.bfloat16)
    grad_out_weight = gram_product(mixed_low, grad_branch)
    grad_mixed = (
        back_product(grad_branch, back_out)
        .astype(jnp.bfloat16)
        .reshape(seq_count, tok_rows, HEADS, HEAD_DIM)
    )
    row_delta = jnp.einsum("sqhd,sqhd->shq", grad_mixed.astype(jnp.float32), mixed)
    keys_again, values_again = (
        lax.all_gather(k_flat, "dp", axis=1, tiled=True),
        lax.all_gather(value_low, "dp", axis=1, tiled=True),
    )
    back_all = jax.vmap(attend_back, in_axes=(0, None, 0, 0, None, 0, 0, 0))
    grad_q_rot, grad_keys_all, grad_values_all = back_all(
        q_rot,
        positions,
        keys_again.reshape(seq_count, seq_len, HEADS, HEAD_DIM),
        values_again.reshape(seq_count, seq_len, HEADS, HEAD_DIM),
        jnp.int32(0),
        grad_mixed,
        log_total,
        row_delta,
    )
    every_query, every_grad = (
        lax.all_gather(q_rot, "dp", axis=1, tiled=True),
        lax.all_gather(grad_mixed, "dp", axis=1, tiled=True),
    )
    every_total, every_delta = (
        lax.all_gather(jnp.transpose(log_total, (0, 2, 1)), "dp", axis=1, tiled=True),
        lax.all_gather(jnp.transpose(row_delta, (0, 2, 1)), "dp", axis=1, tiled=True),
    )
    every_position = jnp.arange(seq_len, dtype=jnp.int32)
    unused_rows, grad_key_mine, grad_value_mine = back_all(
        every_query,
        every_position,
        k_flat.reshape(seq_count, tok_rows, HEADS, HEAD_DIM),
        value_low.reshape(seq_count, tok_rows, HEADS, HEAD_DIM),
        key_offset,
        every_grad,
        jnp.transpose(every_total, (0, 2, 1)),
        jnp.transpose(every_delta, (0, 2, 1)),
    )
    grad_query = (
        rotate(grad_q_rot * scaling, cosine, -sine)
        .reshape(all_rows, model_width)
        .astype(jnp.bfloat16)
    )
    grad_key = (
        rotate(grad_key_mine.reshape(seq_count, tok_rows, HEADS, HEAD_DIM), cosine, -sine)
        .reshape(all_rows, model_width)
        .astype(jnp.bfloat16)
    )
    grad_val = grad_value_mine.reshape(all_rows, model_width).astype(jnp.bfloat16)
    grad_query_weight = gram_product(attn_in, grad_query)
    grad_key_weight = gram_product(attn_in, grad_key)
    grad_value_weight = gram_product(attn_in, grad_val)
    grad_attn_in = (
        back_product(grad_query, back_query)
        + back_product(grad_key, back_key)
        + back_product(grad_val, back_value)
    )
    grad_gain_one = jnp.sum(grad_attn_in * normed_one, axis=0)
    grad_bias_one = jnp.sum(grad_attn_in, axis=0)
    grad_inputs = grad_hidden + norm_backward(
        grad_attn_in, normed_one, inverse_one, back_gain_one.astype(jnp.float32)
    )
    (
        sum_gain_one,
        sum_bias_one,
        sum_query,
        sum_key,
        sum_value,
        sum_out,
        sum_gain_two,
        sum_bias_two,
        sum_up,
        sum_up_bias,
        sum_down,
        sum_down_bias,
    ) = (
        lax.psum_scatter(grad_gain_one, ("dp", "fsdp"), scatter_dimension=0, tiled=True),
        lax.psum_scatter(grad_bias_one, ("dp", "fsdp"), scatter_dimension=0, tiled=True),
        lax.psum_scatter(grad_query_weight, ("dp", "fsdp"), scatter_dimension=0, tiled=True),
        lax.psum_scatter(grad_key_weight, ("dp", "fsdp"), scatter_dimension=0, tiled=True),
        lax.psum_scatter(grad_value_weight, ("dp", "fsdp"), scatter_dimension=0, tiled=True),
        lax.psum_scatter(grad_out_weight, ("dp", "fsdp"), scatter_dimension=0, tiled=True),
        lax.psum_scatter(grad_gain_two, ("dp", "fsdp"), scatter_dimension=0, tiled=True),
        lax.psum_scatter(grad_bias_two, ("dp", "fsdp"), scatter_dimension=0, tiled=True),
        lax.psum_scatter(grad_up_weight, ("dp", "fsdp"), scatter_dimension=0, tiled=True),
        lax.psum_scatter(grad_up_bias, ("dp", "fsdp"), scatter_dimension=0, tiled=True),
        lax.psum_scatter(grad_down_weight, ("dp", "fsdp"), scatter_dimension=0, tiled=True),
        lax.psum_scatter(grad_down_bias, ("dp", "fsdp"), scatter_dimension=0, tiled=True),
    )
    return (
        activations,
        grad_inputs.astype(jnp.bfloat16).reshape(seq_count, tok_rows, model_width),
        sum_gain_one,
        sum_bias_one,
        sum_query,
        sum_key,
        sum_value,
        sum_out,
        sum_gain_two,
        sum_bias_two,
        sum_up,
        sum_up_bias,
        sum_down,
        sum_down_bias,
    )


def solution(mesh):
    placed = (
        P("fsdp", "dp", None),
        P(None, "fsdp", "dp", None),
        P(("dp", "fsdp")),
        P(("dp", "fsdp")),
        P(("dp", "fsdp"), None),
        P(("dp", "fsdp"), None),
        P(("dp", "fsdp"), None),
        P(("dp", "fsdp"), None),
        P(("dp", "fsdp")),
        P(("dp", "fsdp")),
        P(("dp", "fsdp"), None),
        P(("dp", "fsdp")),
        P(("dp", "fsdp"), None),
        P(("dp", "fsdp")),
    )
    return jax.shard_map(
        local,
        mesh=mesh,
        in_specs=placed,
        out_specs=(
            P(None, "fsdp", "dp", None),
            P("fsdp", "dp", None),
            P(("dp", "fsdp")),
            P(("dp", "fsdp")),
            P(("dp", "fsdp"), None),
            P(("dp", "fsdp"), None),
            P(("dp", "fsdp"), None),
            P(("dp", "fsdp"), None),
            P(("dp", "fsdp")),
            P(("dp", "fsdp")),
            P(("dp", "fsdp"), None),
            P(("dp", "fsdp")),
            P(("dp", "fsdp"), None),
            P(("dp", "fsdp")),
        ),
        check_vma=False,
    )
```

profile of v0, /device:TPU:0, one launch (start us, length us, event | category | flops | bytes accessed | tf_op | source)
XLA Modules:
  0.0 2014.2 jit_solution(10184812258126124270)
XLA Ops:
  14.6 43.2 %all-reduce.13 = (bf16[1536]{0:T(1024)(128)(2,1)S(1)}, bf16[1536]{0:T(1024)(128)(2,1)S(1)}, bf16[1536]{0:T(1024)(128)(2,1)S(1)}, bf16[1536]{0:T(1024)(128)(2,1)S...) all-reduce(bf16[1536]{0:T(1024)(128)(2,1)S(1)} %dynamic-update-slic, ...), channel_id=1, replica_groups=mesh['dp'=4,'fsdp'=8] {'dp','fsdp'}, use_global_device_ids=true, to_apply=%add.1 | all-reduce | flops 13824 | bytes 55296
  60.7 16.9 all-gather.12.cloned.1.call-done
  83.6 59.6 %all-gather.18.cloned.1.call-done = bf16[1536,1536]{1,0:T(8,128)(2,1)} async-done(((bf16[48,1536]{1,0:T(8,128)(2,1)}), bf16[1536,1536]{1,0:T(8,128)(2,1)}) %all-gather.18.cloned.1.call-update) | async-done | bytes 4718608 | tf_op jit(solution)/shard_map/all_gather | solution.py:209
  149.8 58.9 %all-gather.14.cloned.1.call-done = bf16[1536,1536]{1,0:T(8,128)(2,1)} async-done(((bf16[48,1536]{1,0:T(8,128)(2,1)}), bf16[1536,1536]{1,0:T(8,128)(2,1)}) %all-gather.14.cloned.1.call-update) | async-done | bytes 4718608 | tf_op jit(solution)/shard_map/all_gather | solution.py:210
  231.3 22.5 %all-gather.30.cloned.1.call-done = bf16[1024,1536]{1,0:T(8,128)(2,1)} async-done(((bf16[256,1536]{1,0:T(8,128)(2,1)}), bf16[1024,1536]{1,0:T(8,128)(2,1)}) %all-gather.30.cloned.1.call-update) | async-done | bytes 3145744 | tf_op jit(solution)/shard_map/all_gather | solution.py:244
  265.9 33.4 %all-gather.16.cloned.1.call-done = bf16[1,1024,1536]{1,2,0:T(8,128)(2,1)} async-done(((bf16[1,256,1536]{1,2,0:T(8,128)(2,1)}), bf16[1,1024,1536]{1,2,0:T(8,128)(2,1)}) %all-gather.16.cloned.1.call-update) | async-done | bytes 3145744 | tf_op jit(solution)/shard_map/all_gather | solution.py:243
  312.7 20.6 %while.40 = (s32[]{:T(128)}, f32[1,12,256]{2,1,0:T(8,128)S(1)}, f32[1,12,256]{2,1,0:T(8,128)S(1)}, s32[2]{0:T(128)S(1)}, bf16[2,1,512,12,128]{4,2,3,1,0:T(8,128)...) while((s32[]{:T(128)}, f32[1,12,256]{2,1,0:T(8,128)S(1)}, ...), condition=%wide.region_5.6_spmd.clone, body=%wide.region_2.5_spmd.clone.sunk | while | flops 412237568 | bytes 15501448 | solution.py:115
  333.4 12.9 while.41
  348.6 17.3 all-gather.20.cloned.1.call-done
  372.6 120.0 %all-gather.22.cloned.1.call-done = bf16[1536,6144]{1,0:T(8,128)(2,1)} async-done(((bf16[48,6144]{1,0:T(8,128)(2,1)}), bf16[1536,6144]{1,0:T(8,128)(2,1)}) %all-gather.22.cloned.1.call-update) | async-done | bytes 18874384 | tf_op jit(solution)/shard_map/all_gather | solution.py:215
  492.6 12.7 multiply_convert_fusion.1
  505.3 113.2 %all-gather.24.cloned.1.call-done = bf16[6144,1536]{1,0:T(8,128)(2,1)} async-done(((bf16[192,1536]{1,0:T(8,128)(2,1)}), bf16[6144,1536]{1,0:T(8,128)(2,1)}) %all-gather.24.cloned.1.call-update) | async-done | bytes 18874384 | tf_op jit(solution)/shard_map/all_gather | solution.py:217
  632.3 13.2 fusion.81
  661.9 12.3 multiply_reduce_fusion
  729.7 28.0 %while.42 = (s32[]{:T(128)}, f32[1,256,12,128]{1,3,2,0:T(8,128)}, bf16[2,1,512,12,128]{4,2,3,1,0:T(8,128)(2,1)S(1)}, s32[2]{0:T(128)}, bf16[1,256,12,128]{3,1,2,...) while((s32[]{:T(128)}, f32[1,256,12,128]{1,3,2,0:T(8,128)}, ...), condition=%wide.region_14.15_spmd.clone, body=%wide.region_13.14_spmd.clone.sunk | while | flops 1218315008 | bytes 22322904 | solution.py:164
  759.5 11.2 fusion.236
  827.3 25.7 %pad_maximum_fusion = f32[1536,6144]{1,0:T(8,128)} fusion(f32[1536,3072]{1,0:T(8,128)} %fusion.246, f32[1536,1536]{1,0:T(8,128)} %fusion.217, f32[1536,768]{1,0:T(8,128)} %fusion.174, f32[1536,768]{1,0:T(8,128)} %fusion.114), kind=kLoop, calls=%fused_computation.66 | loop fusion | flops 28311552 | bytes 75497472 | tf_op jit(solution)/shard_map/concatenate | solution.py:312
  886.2 27.6 %pad_maximum_fusion.1 = f32[6144,1536]{1,0:T(8,128)} fusion(f32[3072,1536]{1,0:T(8,128)} %fusion.214, f32[1536,1536]{1,0:T(8,128)} %fusion.228, f32[768,1536]{1,0:T(8,128)} %fusion.180, f32[768,1536]{1,0:T(8,128)} %fusion.122), kind=kLoop, calls=%fused_computation.67 | loop fusion | flops 28311552 | bytes 75497472 | tf_op jit(solution)/shard_map/concatenate | solution.py:314
  954.0 40.2 %all-reduce.12 = (f32[1536]{0:T(1024)S(1)}, f32[1536]{0:T(1024)S(1)}, f32[1536]{0:T(1024)S(1)}, f32[1536]{0:T(1024)S(1)}, f32[6144]{0:T(1024)S(1)}, /*index=5*/f32[1536]{0:T(1024)S(1)}) all-reduce(f32[1536]{0:T(1024)S(1)} %get-tuple-element.397, ...), channel_id=3, replica_groups=mesh['dp'=4,'fsdp'=8] {'dp','fsdp'}, use_global_device_ids=true, to_apply=%region_18.19.clone | all-reduce | flops 13824 | bytes 110592
  1000.8 12.3 reduce-scatter.7.cloned.1.call-done
  1013.0 141.1 %reduce-scatter.9.cloned.1.call-done = f32[48,1536]{1,0:T(8,128)} async-done(((f32[1536,1536]{1,0:T(8,128)}), f32[48,1536]{1,0:T(8,128)}) %reduce-scatter.9.cloned.1.call-update) | async-done | bytes 294928 | tf_op jit(solution)/shard_map/reduce_scatter | solution.py:403
  1154.1 142.0 %reduce-scatter.11.cloned.1.call-done = f32[48,1536]{1,0:T(8,128)} async-done(((f32[1536,1536]{1,0:T(8,128)}), f32[48,1536]{1,0:T(8,128)}) %reduce-scatter.11.cloned.1.call-update) | async-done | bytes 294928 | tf_op jit(solution)/shard_map/reduce_scatter | solution.py:404
  1296.1 354.9 %reduce-scatter.15.cloned.1.call-done = f32[48,6144]{1,0:T(8,128)} async-done(((f32[1536,6144]{1,0:T(8,128)}), f32[48,6144]{1,0:T(8,128)}) %reduce-scatter.15.cloned.1.call-update) | async-done | bytes 1179664 | tf_op jit(solution)/shard_map/reduce_scatter | solution.py:408
  1651.0 356.2 %reduce-scatter.17.cloned.1.call-done = f32[192,1536]{1,0:T(8,128)} async-done(((f32[6144,1536]{1,0:T(8,128)}), f32[192,1536]{1,0:T(8,128)}) %reduce-scatter.17.cloned.1.call-update) | async-done | bytes 1179664 | tf_op jit(solution)/shard_map/reduce_scatter | solution.py:410
  (361 shorter events, 363.7 us)
Async XLA Ops:
  7.2 70.4 %all-gather.12.cloned.1.call-start = ((), (), s32[]{:S(2)}) async-start(), calls=%async_computation.6 | async-start | bytes 4866048 | tf_op jit(solution)/shard_map/all_gather | solution.py:211
  7.9 135.2 %all-gather.18.cloned.1.call-start = ((), (), s32[]{:S(2)}) async-start(), calls=%async_computation.9 | async-start | bytes 4866048 | tf_op jit(solution)/shard_map/all_gather | solution.py:209
  8.7 200.0 %all-gather.14.cloned.1.call-start = ((), (), s32[]{:S(2)}) async-start(), calls=%async_computation.7 | async-start | bytes 4866048 | tf_op jit(solution)/shard_map/all_gather | solution.py:210
  9.4 244.4 %all-gather.30.cloned.1.call-start = ((), (), s32[]{:S(2)}) async-start(), calls=%async_computation.21 | async-start | bytes 3932160 | tf_op jit(solution)/shard_map/all_gather | solution.py:244
  57.7 162.1 %copy-start.53 = (f32[1536]{0:T(1024)}, f32[1536]{0:T(1024)S(1)}, u32[]{:S(2)}) copy-start(f32[1536]{0:T(1024)S(1)} %convert_element_type.233) | copy-start | bytes 18436
  57.7 162.1 %copy-start.51 = (f32[1536]{0:T(1024)}, f32[1536]{0:T(1024)S(1)}, u32[]{:S(2)}) copy-start(f32[1536]{0:T(1024)S(1)} %convert_element_type.232) | copy-start | bytes 18436
  59.2 160.7 %copy-start.55 = (f32[256]{0:T(256)}, f32[256]{0:T(256)S(1)}, u32[]{:S(2)}) copy-start(f32[256]{0:T(256)S(1)} %broadcast_multiply_fusion.6) | copy-start | bytes 3076
  60.7 159.2 %copy-start.62 = (f32[256]{0:T(256)}, f32[256]{0:T(256)S(1)}, u32[]{:S(2)}) copy-start(f32[256]{0:T(256)S(1)} %add_rsqrt_fusion.1) | copy-start | bytes 3076
  82.6 216.8 %all-gather.16.cloned.1.call-start = ((), (), s32[]{:S(2)}) async-start(), calls=%async_computation.8 | async-start | bytes 3932160 | tf_op jit(solution)/shard_map/all_gather | solution.py:243
  83.6 137.9 %copy-start.45 = (f32[256,64]{0,1:T(8,128)}, f32[256,64]{0,1:T(8,128)S(1)}, u32[]{:S(2)}) copy-start(f32[256,64]{0,1:T(8,128)S(1)} %get-tuple-element.497) | copy-start | bytes 196612
  224.8 141.2 %all-gather.20.cloned.1.call-start = ((), (), s32[]{:S(2)}) async-start(), calls=%async_computation.10 | async-start | bytes 4866048 | tf_op jit(solution)/shard_map/all_gather | solution.py:212
  225.4 267.2 %all-gather.22.cloned.1.call-start = ((), (), s32[]{:S(2)}) async-start(), calls=%async_computation.11 | async-start | bytes 19464192 | tf_op jit(solution)/shard_map/all_gather | solution.py:215
  226.1 392.4 %all-gather.24.cloned.1.call-start = ((), (), s32[]{:S(2)}) async-start(), calls=%async_computation.12 | async-start | bytes 19464192 | tf_op jit(solution)/shard_map/all_gather | solution.py:217
  226.9 486.0 %all-gather.26.cloned.1.call-start = ((), (), s32[]{:S(2)}) async-start(), calls=%async_computation.13 | async-start | bytes 3932160 | tf_op jit(solution)/shard_map/all_gather | solution.py:344
  230.8 528.7 %all-gather.28.cloned.1.call-start = ((), (), s32[]{:S(2)}) async-start(), calls=%async_computation.14 | async-start | bytes 3932160 | tf_op jit(solution)/shard_map/all_gather | solution.py:345
  346.2 24.0 %copy-start.69 = (s32[2]{0:T(128)}, s32[2]{0:T(128)S(1)}, u32[]{:S(2)}) copy-start(s32[2]{0:T(128)S(1)} %get-tuple-element.830) | copy-start | bytes 28
  684.9 315.9 %reduce-scatter.13.cloned.1.call-start = ((), (), s32[]{:S(2)}) async-start(), calls=%async_computation.18 | async-start | bytes 9732096 | tf_op jit(solution)/shard_map/reduce_scatter | solution.py:405
  691.7 321.3 %reduce-scatter.7.cloned.1.call-start = ((), (), s32[]{:S(2)}) async-start(), calls=%async_computation.15 | async-start | bytes 9732096 | tf_op jit(solution)/shard_map/reduce_scatter | solution.py:402
  778.9 375.2 %reduce-scatter.9.cloned.1.call-start = ((), (), s32[]{:S(2)}) async-start(), calls=%async_computation.16 | async-start | bytes 9732096 | tf_op jit(solution)/shard_map/reduce_scatter | solution.py:403
  785.1 511.1 %reduce-scatter.11.cloned.1.call-start = ((), (), s32[]{:S(2)}) async-start(), calls=%async_computation.17 | async-start | bytes 9732096 | tf_op jit(solution)/shard_map/reduce_scatter | solution.py:404
  800.4 850.7 %reduce-scatter.15.cloned.1.call-start = ((), (), s32[]{:S(2)}) async-start(), calls=%async_computation.19 | async-start | bytes 38928384 | tf_op jit(solution)/shard_map/reduce_scatter | solution.py:408
  853.0 1154.2 %reduce-scatter.17.cloned.1.call-start = ((), (), s32[]{:S(2)}) async-start(), calls=%async_computation.20 | async-start | bytes 38928384 | tf_op jit(solution)/shard_map/reduce_scatter | solution.py:410
  861.0 20.4 %copy-start.47 = (bf16[256,768]{1,0:T(8,128)(2,1)}, bf16[256,768]{1,0:T(8,128)(2,1)S(1)}, u32[]{:S(2)}) copy-start(bf16[256,768]{1,0:T(8,128)(2,1)S(1)} %multiply_convert_fusion.7) | copy-start | bytes 1179652
  951.0 46.8 %copy-start.8 = (f32[256,1536]{1,0:T(8,128)S(1)}, f32[256,1536]{1,0:T(8,128)}, u32[]{:S(2)}) copy-start(f32[256,1536]{1,0:T(8,128)} %copy-done.7) | copy-start | bytes 4718596
  (72 other events, 357.2 us)
Sparse Core Ops, SparseCore 0:
  11.0 66.5 all-gather.11
  80.6 62.4 all-gather.17
  146.2 62.4 all-gather.13
  210.9 42.7 all-gather.29
  255.4 43.8 all-gather.15
  302.2 63.7 all-gather.19
  369.0 123.5 all-gather.21
  495.6 122.8 all-gather.23
  620.3 41.9 all-gather.25
  685.0 43.2 all-gather.27
  734.8 135.5 reduce-scatter.12
  877.8 135.1 reduce-scatter.6
  1019.5 134.5 reduce-scatter.8
  1161.5 134.6 reduce-scatter.10
  1303.0 347.9 reduce-scatter.14
  1659.0 348.1 reduce-scatter.16
where the time goes:
time: 2020 us; the launch traced here: 2010 us
  waiting for transfers between devices  1450 us (72%)
  matrix products  255 us (13%)
  other arithmetic  105 us (5%)
  blocking collectives  101 us (5%)
  local copies, waits for them, and re-layouts  83.6 us (4%)
    reduce_scatter x1, waiting for transfers between devices, local(): lax.psum_scatter(grad_down_weight, ('dp', 'fsdp'), scatter_dimension=0, t...  356 us
    reduce_scatter x1, waiting for transfers between devices, local(): lax.psum_scatter(grad_up_weight, ('dp', 'fsdp'), scatter_dimension=0, til...  355 us
    reduce_scatter x1, waiting for transfers between devices, local(): lax.psum_scatter(grad_value_weight, ('dp', 'fsdp'), scatter_dimension=0,...  142 us
    reduce_scatter x1, waiting for transfers between devices, local(): lax.psum_scatter(grad_key_weight, ('dp', 'fsdp'), scatter_dimension=0, ti...  141 us
    all_gather x1, waiting for transfers between devices, local(): lax.all_gather(up_weight, ('dp', 'fsdp'), axis=0, tiled=True)  120 us
    all_gather x1, waiting for transfers between devices, local(): lax.all_gather(down_weight, ('dp', 'fsdp'), axis=0, tiled=True)  113 us
    unnamed x2, blocking collectives  83.4 us
    dot_general x12, matrix products, gram_product(): lax.dot_general(left, right, (((0,), (0,)), ((), ())), preferred_element_...  67.4 us
  transfers between devices with their start and end apart: 16, of which 13 were waited for; matrix products, arithmetic and copies ran while one was open for 22% of the time, Pallas kernels for 0%

commit v1 on v0

--- a/solution.py
+++ b/solution.py
@@ -1,3 +1,4 @@
+import functools
 import math
 
 import jax
@@ -174,7 +175,7 @@
     )
 
 
-def local(
+def local_gathered(
     tokens,
     cotangent,
     norm1_gain,
@@ -428,6 +429,241 @@
     )
 
 
+def piece_blocks(ranks):
+    piece_count = max(2 ** (GRAN - 1), ranks)
+    width = FF // piece_count
+    edges = [FF // 2 ** (GRAN - 1 - level_idx) for level_idx in range(GRAN)]
+    blocks = []
+    for piece in range(piece_count):
+        blocks.append(next(b for b in range(GRAN) if piece * width < edges[b]))
+    per_rank = piece_count // ranks
+    return [blocks[rank * per_rank : (rank + 1) * per_rank] for rank in range(ranks)], width
+
+
+def local_split(ranks, shards, *arguments):
+    (
+        tokens,
+        cotangent,
+        norm1_gain,
+        norm1_bias,
+        query_weight,
+        key_weight,
+        value_weight,
+        out_weight,
+        norm2_gain,
+        norm2_bias,
+        up_weight,
+        up_bias,
+        down_weight,
+        down_bias,
+    ) = arguments
+    model_width = tokens.shape[2]
+    tok_rows = tokens.shape[1]
+    seq_len = tok_rows * ranks
+    own = query_weight.shape[0]
+    heads = HEADS // ranks
+    head_cols = heads * HEAD_DIM
+    ff_cols = FF // ranks
+    scaling = HEAD_DIM ** (-0.5)
+    rank = lax.axis_index("dp")
+
+    small = jnp.concatenate([norm1_gain, norm1_bias, norm2_gain, norm2_bias, down_bias, up_bias])
+    small = lax.all_gather(small, ("dp", "fsdp"), axis=0, tiled=False).astype(jnp.float32)
+    gain_one, bias_one, gain_two, bias_two, b_down = (
+        small[:, i * own : (i + 1) * own].reshape(model_width) for i in range(5)
+    )
+    b_up_all = small[:, 5 * own :].reshape(ranks, ff_cols)
+    b_up = lax.dynamic_index_in_dim(b_up_all, rank, 0, keepdims=False)
+
+    def to_parts(weight):
+        return weight.reshape(own, ranks, -1).transpose(1, 0, 2)
+
+    mixed_weights = jnp.concatenate(
+        [to_parts(w) for w in (query_weight, key_weight, value_weight)], axis=2
+    )
+
+    def spread(parts):
+        parts = lax.all_to_all(parts, "dp", split_axis=0, concat_axis=0)
+        parts = lax.all_gather(parts, "fsdp", axis=1, tiled=False)
+        return parts.reshape(model_width, -1)
+
+    w_qkv = spread(mixed_weights)
+    w_out = lax.all_gather(out_weight, "fsdp", axis=0, tiled=True)
+    w_up = spread(to_parts(up_weight))
+    w_down = lax.all_gather(down_weight, "fsdp", axis=0, tiled=True)
+
+    own_tokens = tokens.reshape(tok_rows, model_width)
+    all_tokens = lax.all_gather(own_tokens, "dp", axis=0, tiled=True).astype(jnp.float32)
+    normed_all, unused = norm_parts(all_tokens)
+    attn_in = (normed_all * gain_one + bias_one).astype(jnp.bfloat16)
+    qkv = product(attn_in, w_qkv)
+    queries = qkv[:, :head_cols].reshape(seq_len, heads, HEAD_DIM)
+    key_raw = qkv[:, head_cols : 2 * head_cols].reshape(seq_len, heads, HEAD_DIM)
+    values = qkv[:, 2 * head_cols :].astype(jnp.bfloat16).reshape(seq_len, heads, HEAD_DIM)
+    positions = jnp.arange(seq_len, dtype=jnp.int32)
+    cosine, sine = rotary_tables(positions.astype(jnp.float32), HEAD_DIM // 2)
+    q_rot = (rotate(queries, cosine, sine) * scaling).astype(jnp.bfloat16)
+    k_rot = rotate(key_raw, cosine, sine).astype(jnp.bfloat16)
+    visible = (positions[:, None] >= positions[None, :])[None]
+
+    def weigh(log_total=None):
+        scores = jnp.einsum("qhd,khd->hqk", q_rot, k_rot, preferred_element_type=jnp.float32)
+        scores = jnp.where(visible, scores, masked_score)
+        if log_total is None:
+            top = jnp.max(scores, axis=-1)
+            log_total = top + jnp.log(jnp.sum(jnp.exp(scores - top[..., None]), axis=-1))
+        return jnp.exp(scores - log_total[..., None]), log_total
+
+    probs, log_total = weigh()
+    mixed = jnp.einsum(
+        "hqk,khd->qhd", probs.astype(jnp.bfloat16), values, preferred_element_type=jnp.float32
+    )
+    mixed_low = mixed.reshape(seq_len, head_cols).astype(jnp.bfloat16)
+
+    def add_up(partial):
+        return lax.psum_scatter(
+            partial.astype(jnp.bfloat16), "dp", scatter_dimension=0, tiled=True
+        ).astype(jnp.float32)
+
+    inputs = own_tokens.astype(jnp.float32)
+    hidden = inputs + add_up(product(mixed_low, w_out))
+    normed_two, inverse_two = norm_parts(hidden)
+    ffn_in_own = (normed_two * gain_two + bias_two).astype(jnp.bfloat16)
+    ffn_in = lax.all_gather(ffn_in_own, "dp", axis=0, tiled=True)
+    preact = product(ffn_in, w_up) + b_up
+    gated = gelu_value(preact).astype(jnp.bfloat16)
+
+    blocks, width = piece_blocks(ranks)
+    pieces = len(blocks[0])
+    terms = jnp.stack(
+        [
+            product(gated[:, i * width : (i + 1) * width], w_down[i * width : (i + 1) * width])
+            .astype(jnp.bfloat16)
+            .reshape(ranks, tok_rows, model_width)
+            for i in range(pieces)
+        ],
+        axis=1,
+    )
+    terms = lax.all_to_all(terms, "dp", split_axis=0, concat_axis=0)
+    total = hidden + b_down
+    result_list = []
+    for level_idx in range(GRAN):
+        for source in range(ranks):
+            for i in range(pieces):
+                if blocks[source][i] == level_idx:
+                    total = total + terms[source, i].astype(jnp.float32)
+        result_list.append(total.astype(jnp.bfloat16))
+    activations = jnp.stack(result_list).reshape(GRAN, 1, tok_rows, model_width)
+
+    grads_out = cotangent.reshape(GRAN, tok_rows, model_width).astype(jnp.float32)
+    suffix = [grads_out[GRAN - 1]]
+    for level_idx in range(GRAN - 2, -1, -1):
+        suffix.insert(0, suffix[0] + grads_out[level_idx])
+    grad_hidden = suffix[0]
+    suffix = [s.astype(jnp.bfloat16) for s in suffix]
+    outgoing = jnp.stack([jnp.stack([suffix[b] for b in blocks[j]]) for j in range(ranks)])
+    incoming = lax.all_to_all(outgoing, "dp", split_axis=0, concat_axis=0)
+    incoming = incoming.transpose(1, 0, 2, 3).reshape(pieces, seq_len, model_width)
+
+    grad_gated = jnp.concatenate(
+        [back_product(incoming[i], w_down[i * width : (i + 1) * width]) for i in range(pieces)],
+        axis=1,
+    )
+    grad_pre_wide = grad_gated * gelu_grad(preact)
+    grad_pre = grad_pre_wide.astype(jnp.bfloat16)
+    grad_up_bias = jnp.sum(grad_pre_wide, axis=0)
+    grad_ffn_in = add_up(back_product(grad_pre, w_up))
+
+    def collect(grad):
+        return lax.psum_scatter(
+            grad.astype(jnp.bfloat16), "fsdp", scatter_dimension=0, tiled=True
+        )
+
+    def collect_columns(grad):
+        columns = grad.shape[1]
+        grad = grad.astype(jnp.bfloat16).reshape(ranks, shards, own, columns)
+        grad = grad.transpose(1, 0, 2, 3).reshape(model_width, columns)
+        grad = lax.psum_scatter(grad, "fsdp", scatter_dimension=0, tiled=True)
+        grad = grad.reshape(ranks, own, columns)
+        grad = lax.all_to_all(grad, "dp", split_axis=0, concat_axis=0)
+        return grad.astype(jnp.float32)
+
+    sum_down = collect(
+        jnp.concatenate(
+            [gram_product(gated[:, i * width : (i + 1) * width], incoming[i]) for i in range(pieces)],
+            axis=0,
+        )
+    ).astype(jnp.float32)
+    sum_up = collect_columns(gram_product(ffn_in, grad_pre))
+    sum_up = sum_up.transpose(1, 0, 2).reshape(own, FF)
+
+    grad_down_bias = jnp.sum(grad_hidden, axis=0)
+    grad_gain_two = jnp.sum(grad_ffn_in * normed_two, axis=0)
+    grad_bias_two = jnp.sum(grad_ffn_in, axis=0)
+    grad_hidden = grad_hidden + norm_backward(grad_ffn_in, normed_two, inverse_two, gain_two)
+    grad_branch = lax.all_gather(grad_hidden.astype(jnp.bfloat16), "dp", axis=0, tiled=True)
+    sum_out = collect(gram_product(mixed_low, grad_branch)).astype(jnp.float32)
+    grad_mixed = (
+        back_product(grad_branch, w_out).astype(jnp.bfloat16).reshape(seq_len, heads, HEAD_DIM)
+    )
+    row_delta = jnp.einsum("qhd,qhd->hq", grad_mixed.astype(jnp.float32), mixed)
+    probs, unused = weigh(log_total)
+    grad_probs = jnp.einsum("qhd,khd->hqk", grad_mixed, values, preferred_element_type=jnp.float32)
+    grad_scores = (probs * (grad_probs - row_delta[..., None])).astype(jnp.bfloat16)
+    grad_q_rot = jnp.einsum(
+        "hqk,khd->qhd", grad_scores, k_rot, preferred_element_type=jnp.float32
+    )
+    grad_k_rot = jnp.einsum(
+        "hqk,qhd->khd", grad_scores, q_rot, preferred_element_type=jnp.float32
+    )
+    grad_values = jnp.einsum(
+        "hqk,qhd->khd", probs.astype(jnp.bfloat16), grad_mixed, preferred_element_type=jnp.float32
+    )
+    grad_qkv = jnp.concatenate(
+        [
+            rotate(grad_q_rot * scaling, cosine, -sine).reshape(seq_len, head_cols),
+            rotate(grad_k_rot, cosine, -sine).reshape(seq_len, head_cols),
+            grad_values.reshape(seq_len, head_cols),
+        ],
+        axis=1,
+    ).astype(jnp.bfloat16)
+    sum_qkv = collect_columns(gram_product(attn_in, grad_qkv)).transpose(1, 0, 2)
+    sum_query, sum_key, sum_value = (
+        sum_qkv[:, :, i * head_cols : (i + 1) * head_cols].reshape(own, model_width)
+        for i in range(3)
+    )
+    grad_attn_in = add_up(back_product(grad_qkv, w_qkv))
+    normed_one, inverse_one = norm_parts(inputs)
+    grad_gain_one = jnp.sum(grad_attn_in * normed_one, axis=0)
+    grad_bias_one = jnp.sum(grad_attn_in, axis=0)
+    grad_inputs = grad_hidden + norm_backward(grad_attn_in, normed_one, inverse_one, gain_one)
+
+    sums = jnp.stack([grad_gain_one, grad_bias_one, grad_gain_two, grad_bias_two, grad_down_bias])
+    sums = lax.psum_scatter(
+        sums.reshape(5, ranks * shards, own).transpose(1, 0, 2).reshape(ranks * shards, 5 * own),
+        ("dp", "fsdp"),
+        scatter_dimension=0,
+        tiled=True,
+    ).reshape(5, own)
+    sum_up_bias = lax.psum_scatter(grad_up_bias, "fsdp", scatter_dimension=0, tiled=True)
+    return (
+        activations,
+        grad_inputs.astype(jnp.bfloat16).reshape(1, tok_rows, model_width),
+        sums[0],
+        sums[1],
+        sum_query,
+        sum_key,
+        sum_value,
+        sum_out,
+        sums[2],
+        sums[3],
+        sum_up,
+        sum_up_bias,
+        sum_down,
+        sums[4],
+    )
+
+
 def solution(mesh):
     placed = (
         P("fsdp", "dp", None),
@@ -445,6 +681,10 @@
         P(("dp", "fsdp"), None),
         P(("dp", "fsdp")),
     )
+    ranks, shards = mesh.shape["dp"], mesh.shape["fsdp"]
+    local = local_gathered
+    if HEADS % ranks == 0:
+        local = functools.partial(local_split, ranks, shards)
     return jax.shard_map(
         local,
         mesh=mesh,

time: 2020 us -> 877 us (0.43)
  waiting for transfers between devices: 1450 us -> 448 us
  matrix products: 255 us -> 120 us
  other arithmetic: 105 us -> 64.7 us
  blocking collectives: 101 us -> 129 us
    reduce_scatter x6 -> x7, waiting for transfers between devices: 1010 us -> 268 us  [the longest x3 170 us: add_up(): lax.psum_scatter(partial.astype(jnp.bfloat16), 'dp', scatter_dimension=0,...]
    all_gather x10 -> x7, waiting for transfers between devices: 442 us -> 151 us  [the longest x2 66.9 us: spread(): parts = lax.all_gather(parts, 'fsdp', axis=1, tiled=False)]
    concatenate x3 -> x2, other arithmetic: 53.3 us -> 2.63 us  [the longest x1 2.44 us: local_split(): jnp.concatenate([gram_product(gated[:, i * width:(i + 1) * width], incomi...]
    dot_general x12 -> x5, matrix products: 67.4 us -> 26.4 us  [gram_product(): lax.dot_general(left, right, (((0,), (0,)), ((), ())), preferred_element_...]
    dot_general x11 -> x6, matrix products: 72.5 us -> 32.8 us  [the longest x1 8.31 us: local_split(): jnp.einsum('hqk,qhd->khd', probs.astype(jnp.bfloat16), grad_mixed, prefer...]
    dot_general x12 -> x5, matrix products: 63.8 us -> 27.5 us  [back_product(): lax.dot_general(left, right, (((1,), (1,)), ((), ())), preferred_element_...]
    all_to_all x0 -> x2, blocking collectives: none -> 32.8 us  [spread(): parts = lax.all_to_all(parts, 'dp', split_axis=0, concat_axis=0)]
    all_to_all x0 -> x4, waiting for transfers between devices: none -> 26.5 us  [the longest x1 18 us: local_split(): incoming = lax.all_to_all(outgoing, 'dp', split_axis=0, concat_axis=0)]
  transfers between devices with their start and end apart: 16 -> 18, of which waited for: 13 -> 13; matrix products, arithmetic and copies ran while one was open for 22% -> 24% of each run, Pallas kernels for 0% -> 0%
where the time goes in v1:
time: 877 us; the launch traced here: 866 us
  waiting for transfers between devices  448 us (51%)
  blocking collectives  129 us (15%)
  matrix products  120 us (14%)
  local copies, waits for them, and re-layouts  67.6 us (8%)
  other arithmetic  64.7 us (7%)
  starting transfers between devices  20.3 us (2%)
  between operations  16 us (2%)
    reduce_scatter x3, waiting for transfers between devices, add_up(): lax.psum_scatter(partial.astype(jnp.bfloat16), 'dp', scatter_dimension=0,...  170 us
    unnamed x3, blocking collectives  96.3 us
    all_gather x2, waiting for transfers between devices, spread(): parts = lax.all_gather(parts, 'fsdp', axis=1, tiled=False)  66.9 us
    reduce_scatter x2, waiting for transfers between devices, collect(): lax.psum_scatter(grad.astype(jnp.bfloat16), 'fsdp', scatter_dimension=0,...  54 us
    reduce_scatter x2, waiting for transfers between devices, collect_columns(): grad = lax.psum_scatter(grad, 'fsdp', scatter_dimension=0, tiled=True)  44.1 us
    all_gather x1, waiting for transfers between devices, local_split(): ffn_in = lax.all_gather(ffn_in_own, 'dp', axis=0, tiled=True)  39.3 us
    dot_general x5, matrix products, product(): return jnp.dot(left, right, preferred_element_type=jnp.float32)  33.3 us
    all_to_all x2, blocking collectives, spread(): parts = lax.all_to_all(parts, 'dp', split_axis=0, concat_axis=0)  32.8 us
  transfers between devices with their start and end apart: 18, of which 13 were waited for; matrix products, arithmetic and copies ran while one was open for 24% of the time, Pallas kernels for 0%

profile of v1, /device:TPU:0, one launch (start us, length us, event | category | flops | bytes accessed | tf_op | source)
XLA Modules:
  0.0 865.6 jit_solution(11439245601962537849)
XLA Ops:
  11.1 12.9 %all_to_all.30 = bf16[4,48,1152]{2,1,0:T(8,128)(2,1)S(1)} all-to-all(bf16[4,48,1152]{2,1,0:T(8,128)(2,1)S(1)} %copy.103), channel_id=1, replica_groups=mesh['dp'=4,'fsdp'=8] {'dp'}, dimensions={0} | all-to-all | bytes 884736 | tf_op jit(solution)/shard_map/all_to_all | solution.py:486
  26.6 40.4 %all-reduce = bf16[13824]{0:T(1024)(128)(2,1)S(1)} all-reduce(bf16[13824]{0:T(1024)(128)(2,1)S(1)} %dynamic-update-slice), channel_id=3, replica_groups=mesh['dp'=4,'fsdp'=8] {'dp','fsdp'}, use_global_device_ids=true, to_apply=%add | all-reduce | flops 13824 | bytes 55296
  74.5 26.4 %all-gather.22.cloned.1.call-done = bf16[4,384,1152]{2,0,1:T(4,128)(2,1)} async-done(((bf16[4,48,1152]{2,0,1:T(4,128)(2,1)}), bf16[4,384,1152]{2,0,1:T(4,128)(2,1)}) %all-gather.22.cloned.1.call-update) | async-done | bytes 3538960 | tf_op jit(solution)/shard_map/all_gather | solution.py:487
  141.7 7.3 exponential_reduce_fusion
  165.2 19.9 %all_to_all.31 = bf16[4,48,1536]{2,1,0:T(8,128)(2,1)S(1)} all-to-all(bf16[4,48,1536]{2,1,0:T(8,128)(2,1)S(1)} %copy.114), channel_id=1, replica_groups=mesh['dp'=4,'fsdp'=8] {'dp'}, dimensions={0} | all-to-all | bytes 1179648 | tf_op jit(solution)/shard_map/all_to_all | solution.py:486
  197.5 54.3 %reduce-scatter.8.cloned.1.call-done = bf16[256,1536]{1,0:T(8,128)(2,1)} async-done(((bf16[1024,1536]{1,0:T(8,128)(2,1)}), bf16[256,1536]{1,0:T(8,128)(2,1)}) %reduce-scatter.8.cloned.1.call-update) | async-done | bytes 786448 | tf_op jit(solution)/shard_map/reduce_scatter | solution.py:524
  256.8 18.0 %all-to-all-done.3 = bf16[4,2,256,1536]{3,2,1,0:T(8,128)(2,1)} async-done(((bf16[4,2,256,1536]{3,2,1,0:T(8,128)(2,1)}), bf16[4,2,256,1536]{3,2,1,0:T(8,128)(2,1)}, u32[]{:S(2)}, u32[]{:S(2)}) %all-to-all-start.3) | async-done | bytes 6291488 | tf_op jit(solution)/shard_map/all_to_all | solution.py:565
  280.8 21.3 %all-gather.16.cloned.1.call-done = bf16[1536,1536]{1,0:T(8,128)(2,1)} async-done(((bf16[192,1536]{1,0:T(8,128)(2,1)}), bf16[1536,1536]{1,0:T(8,128)(2,1)}) %all-gather.16.cloned.1.call-update) | async-done | bytes 4718608 | tf_op jit(solution)/shard_map/all_gather | solution.py:493
  302.1 7.2 fusion.20
  313.6 40.5 %all-gather.24.cloned.1.call-done = bf16[4,384,1536]{2,0,1:T(4,128)(2,1)} async-done(((bf16[4,48,1536]{2,0,1:T(4,128)(2,1)}), bf16[4,384,1536]{2,0,1:T(4,128)(2,1)}) %all-gather.24.cloned.1.call-update) | async-done | bytes 4718608 | tf_op jit(solution)/shard_map/all_gather | solution.py:487
  359.5 39.3 %all-gather.14.cloned.1.call-done = bf16[1024,1536]{1,0:T(8,128)(2,1)} async-done(((bf16[256,1536]{1,0:T(8,128)(2,1)}), bf16[1024,1536]{1,0:T(8,128)(2,1)}) %all-gather.14.cloned.1.call-update) | async-done | bytes 3145744 | tf_op jit(solution)/shard_map/all_gather | solution.py:532
  398.8 14.2 %fusion.72 = (f32[1536]{0:T(1024)S(1)}, bf16[1024,1536]{1,0:T(8,128)(2,1)S(1)}, bf16[1024,1536]{1,0:T(8,128)(2,1)}) fusion(f32[1536]{0:T(1024)S(1)} %dynamic-slice_reduce_fusion, f32[1024,768]{1,0:T(8,128)} %fusion.20, f32[1024,768]{1,0:T(8,128)} %fusion.23, bf16[1024,1536]{1,0:T(8,128)(2,1)} %all-gather.14.cloned.1.call-done, bf16[1536,1536]{1,0:T(8,128)(2,1)} %bitcast.258), kind=kOutput, calls=%fused_computation.178 | convolution fusion | flops 4869585408 | bytes 20459520 | tf_op jit(solution)/shard_map/dot_general | solution.py:20
  439.6 72.3 %reduce-scatter.10.cloned.1.call-done = bf16[256,1536]{1,0:T(8,128)(2,1)} async-done(((bf16[1024,1536]{1,0:T(8,128)(2,1)}), bf16[256,1536]{1,0:T(8,128)(2,1)}) %reduce-scatter.10.cloned.1.call-update) | async-done | bytes 786448 | tf_op jit(solution)/shard_map/reduce_scatter | solution.py:524
  514.2 8.5 all-to-all-done.2
  527.9 7.8 convolution_convert_fusion
  549.1 23.7 %all-gather.18.cloned.1.call-done = bf16[1024,1536]{1,0:T(8,128)(2,1)} async-done(((bf16[256,1536]{1,0:T(8,128)(2,1)}), bf16[1024,1536]{1,0:T(8,128)(2,1)}) %all-gather.18.cloned.1.call-update) | async-done | bytes 3145744 | tf_op jit(solution)/shard_map/all_gather | solution.py:604
  580.6 7.4 multiply_convert_fusion
  604.7 8.3 convolution_convert_fusion.10
  631.8 17.4 %all-reduce.2 = f32[1536]{0:T(1024)S(1)} all-reduce(f32[1536]{0:T(1024)S(1)} %get-tuple-element.79), channel_id=13, replica_groups=mesh['dp'=4,'fsdp'=8] {'fsdp'}, use_global_device_ids=true, to_apply=%region_25.26.clone | all-reduce | flops 1536 | bytes 12288
  660.6 25.3 %reduce-scatter.20.cloned.1.call-done = bf16[192,1536]{1,0:T(8,128)(2,1)} async-done(((bf16[1536,1536]{1,0:T(8,128)(2,1)}), bf16[192,1536]{1,0:T(8,128)(2,1)}) %reduce-scatter.20.cloned.1.call-update) | async-done | bytes 589840 | tf_op jit(solution)/shard_map/reduce_scatter | solution.py:578
  690.6 28.6 %reduce-scatter.16.cloned.1.call-done = bf16[48,1536]{1,0:T(8,128)(2,1)} async-done(((bf16[384,1536]{1,0:T(8,128)(2,1)}), bf16[48,1536]{1,0:T(8,128)(2,1)}) %reduce-scatter.16.cloned.1.call-update) | async-done | bytes 147472 | tf_op jit(solution)/shard_map/reduce_scatter | solution.py:578
  720.9 43.5 %reduce-scatter.12.cloned.1.call-done = bf16[256,1536]{1,0:T(8,128)(2,1)} async-done(((bf16[1024,1536]{1,0:T(8,128)(2,1)}), bf16[256,1536]{1,0:T(8,128)(2,1)}) %reduce-scatter.12.cloned.1.call-update) | async-done | bytes 786448 | tf_op jit(solution)/shard_map/reduce_scatter | solution.py:524
  766.3 44.1 %reduce-scatter.14.cloned.1.call-done = bf16[192,1152]{1,0:T(8,128)(2,1)} async-done(((bf16[1536,1152]{1,0:T(8,128)(2,1)}), bf16[192,1152]{1,0:T(8,128)(2,1)}) %reduce-scatter.14.cloned.1.call-update) | async-done | bytes 442384 | tf_op jit(solution)/shard_map/reduce_scatter | solution.py:586
  817.1 38.5 %all-reduce.1 = f32[32,240]{1,0:T(8,128)S(1)} all-reduce(f32[32,240]{1,0:T(8,128)S(1)} %reshape.358), channel_id=9, replica_groups=mesh['dp'=4,'fsdp'=8] {'dp','fsdp'}, use_global_device_ids=true, to_apply=%region_20.21.clone | all-reduce | flops 7680 | bytes 61440
  (260 shorter events, 222.4 us)
Async XLA Ops:
  7.2 63.3 %all-gather.20.cloned.1.call-start = ((), (), s32[]{:S(2)}) async-start(), calls=%async_computation.24 | async-start | bytes 3932160 | tf_op jit(solution)/shard_map/all_gather | solution.py:496
  8.0 92.9 %all-gather.22.cloned.1.call-start = ((), (), s32[]{:S(2)}) async-start(), calls=%async_computation.25 | async-start | bytes 3981312 | tf_op jit(solution)/shard_map/all_gather | solution.py:487
  25.0 130.7 %all-gather.12.cloned.1.call-start = ((), (), s32[]{:S(2)}) async-start(), calls=%async_computation.13 | async-start | bytes 1327104 | tf_op jit(solution)/shard_map/all_gather | solution.py:491
  25.8 226.0 %reduce-scatter.8.cloned.1.call-start = ((), (), s32[]{:S(2)}) async-start(), calls=%async_computation.14 | async-start | bytes 3932160 | tf_op jit(solution)/shard_map/reduce_scatter | solution.py:524
  26.1 106.8 %copy-start.3 = (pred[1024,1024]{0,1:T(8,128)(4,1)}, pred[1024,1024]{0,1:T(8,128)(4,1)S(1)}, u32[]{:S(2)}) copy-start(pred[1024,1024]{0,1:T(8,128)(4,1)S(1)} %iota_compare_fusion) | copy-start | bytes 3145732
  67.3 36.2 %copy-start.31 = (f32[1536]{0:T(1024)}, f32[1536]{0:T(1024)S(1)}, u32[]{:S(2)}) copy-start(f32[1536]{0:T(1024)S(1)} %mul.453) | copy-start | bytes 18436
  67.4 36.1 %copy-start.35 = (f32[1536]{0:T(1024)}, f32[1536]{0:T(1024)S(1)}, u32[]{:S(2)}) copy-start(f32[1536]{0:T(1024)S(1)} %add.183) | copy-start | bytes 18436
  70.5 58.6 %copy-start.14 = (f32[1024,64]{1,0:T(8,128)}, f32[1024,64]{1,0:T(8,128)S(1)}, u32[]{:S(2)}) copy-start(f32[1024,64]{1,0:T(8,128)S(1)} %get-tuple-element.131) | copy-start | bytes 786436
  160.7 141.4 %all-gather.16.cloned.1.call-start = ((), (), s32[]{:S(2)}) async-start(), calls=%async_computation.16 | async-start | bytes 5308416 | tf_op jit(solution)/shard_map/all_gather | solution.py:493
  161.3 192.8 %all-gather.24.cloned.1.call-start = ((), (), s32[]{:S(2)}) async-start(), calls=%async_computation.26 | async-start | bytes 5308416 | tf_op jit(solution)/shard_map/all_gather | solution.py:487
  191.9 59.9 %copy-start.1 = (bf16[1,256,1536]{2,1,0:T(8,128)(2,1)S(1)}, bf16[1,256,1536]{2,1,0:T(8,128)(2,1)}, u32[]{:S(2)}) copy-start(bf16[1,256,1536]{2,1,0:T(8,128)(2,1)} %param.14) | copy-start | bytes 2359300
  191.9 82.9 %all-to-all-start.3 = ((bf16[4,2,256,1536]{3,2,1,0:T(8,128)(2,1)}), bf16[4,2,256,1536]{3,2,1,0:T(8,128)(2,1)}, u32[]{:S(2)}, u32[]{:S(2)}) async-start(bf16[4,2,256,1536]{3,2,1,0:T(8,128)(2,1)} %pad_maximum_fusion.1), calls=%async_computation.4 | async-start | bytes 12582912 | tf_op jit(solution)/shard_map/all_to_all | solution.py:565
  197.3 201.5 %all-gather.14.cloned.1.call-start = ((), (), s32[]{:S(2)}) async-start(), calls=%async_computation.15 | async-start | bytes 3932160 | tf_op jit(solution)/shard_map/all_gather | solution.py:532
  256.2 255.7 %reduce-scatter.10.cloned.1.call-start = ((), (), s32[]{:S(2)}) async-start(), calls=%async_computation.17 | async-start | bytes 3932160 | tf_op jit(solution)/shard_map/reduce_scatter | solution.py:524
  433.9 88.9 %all-to-all-start.2 = ((bf16[4,2,256,1536]{3,2,1,0:T(8,128)(2,1)}), bf16[4,2,256,1536]{3,2,1,0:T(8,128)(2,1)}, u32[]{:S(2)}, u32[]{:S(2)}) async-start(bf16[4,2,256,1536]{3,2,1,0:T(8,128)(2,1)} %pad_maximum_fusion), calls=%async_computation.3 | async-start | bytes 12582912 | tf_op jit(solution)/shard_map/all_to_all | solution.py:547
  439.1 133.6 %all-gather.18.cloned.1.call-start = ((), (), s32[]{:S(2)}) async-start(), calls=%async_computation.18 | async-start | bytes 3932160 | tf_op jit(solution)/shard_map/all_gather | solution.py:604
  527.8 125.3 %reduce-scatter.18.cloned.1.call-start = ((), (), s32[]{:S(2)}) async-start(), calls=%async_computation.22 | async-start | bytes 5308416 | tf_op jit(solution)/shard_map/reduce_scatter | solution.py:586
  538.2 147.8 %reduce-scatter.20.cloned.1.call-start = ((), (), s32[]{:S(2)}) async-start(), calls=%async_computation.23 | async-start | bytes 5308416 | tf_op jit(solution)/shard_map/reduce_scatter | solution.py:578
  548.8 170.4 %reduce-scatter.16.cloned.1.call-start = ((), (), s32[]{:S(2)}) async-start(), calls=%async_computation.21 | async-start | bytes 1327104 | tf_op jit(solution)/shard_map/reduce_scatter | solution.py:578
  593.7 170.7 %reduce-scatter.12.cloned.1.call-start = ((), (), s32[]{:S(2)}) async-start(), calls=%async_computation.19 | async-start | bytes 3932160 | tf_op jit(solution)/shard_map/reduce_scatter | solution.py:524
  619.8 190.6 %reduce-scatter.14.cloned.1.call-start = ((), (), s32[]{:S(2)}) async-start(), calls=%async_computation.20 | async-start | bytes 3981312 | tf_op jit(solution)/shard_map/reduce_scatter | solution.py:586
  653.1 35.1 %all-to-all-start.5 = ((bf16[4,48,1536]{2,1,0:T(8,128)(2,1)}), bf16[4,48,1536]{2,1,0:T(8,128)(2,1)}, u32[]{:S(2)}, u32[]{:S(2)}) async-start(bf16[4,48,1536]{2,1,0:T(8,128)(2,1)} %bitcast.284), calls=%async_computation.11 | async-start | bytes 1179648 | tf_op jit(solution)/shard_map/all_to_all | solution.py:588
  688.2 125.8 %copy-start.11 = (f32[256,1536]{1,0:T(8,128)S(1)}, f32[256,1536]{1,0:T(8,128)}, u32[]{:S(2)}) copy-start(f32[256,1536]{1,0:T(8,128)} %get-tuple-element.84) | copy-start | bytes 4718596
  810.4 45.8 %all-to-all-start.4 = ((bf16[4,48,1152]{2,1,0:T(8,128)(2,1)}), bf16[4,48,1152]{2,1,0:T(8,128)(2,1)S(1)}, u32[]{:S(2)}, u32[]{:S(2)}) async-start(bf16[4,48,1152]{2,1,0:T(8,128)(2,1)} %bitcast.286), calls=%async_computation.8 | async-start | bytes 884736 | tf_op jit(solution)/shard_map/all_to_all | solution.py:588
  (47 other events, 412.0 us)
Sparse Core Ops, SparseCore 0:
  9.9 47.3 all-gather.19
  59.4 41.4 all-gather.21
  102.5 21.5 all-gather.11
  160.8 90.9 reduce-scatter.7
  253.3 48.7 all-gather.15
  303.6 50.5 all-gather.23
  356.0 42.7 all-gather.13
  421.4 90.5 reduce-scatter.9
  527.9 44.7 all-gather.17
  574.9 54.9 reduce-scatter.17
  632.2 53.7 reduce-scatter.19
  688.1 31.0 reduce-scatter.15
  722.2 42.1 reduce-scatter.11
  766.6 43.7 reduce-scatter.13

commit v2 on v1

--- a/solution.py
+++ b/solution.py
@@ -4,6 +4,8 @@
 import jax
 import jax.numpy as jnp
 from jax import lax
+from jax.experimental import pallas as pl
+from jax.experimental.pallas import tpu as pltpu
 from jax.sharding import PartitionSpec as P
 
 HEADS = 12
@@ -429,18 +431,490 @@
     )
 
 
-def piece_blocks(ranks):
-    piece_count = max(2 ** (GRAN - 1), ranks)
-    width = FF // piece_count
-    edges = [FF // 2 ** (GRAN - 1 - level_idx) for level_idx in range(GRAN)]
-    blocks = []
-    for piece in range(piece_count):
-        blocks.append(next(b for b in range(GRAN) if piece * width < edges[b]))
-    per_rank = piece_count // ranks
-    return [blocks[rank * per_rank : (rank + 1) * per_rank] for rank in range(ranks)], width
+MESH = pl.DeviceIdType.MESH
+
+
+class Place:
+    def __init__(self, chips):
+        self.chips = chips
+        self.rank = lax.axis_index("dp")
+        self.shard = lax.axis_index("fsdp")
+        self.z = lax.div(self.shard, 2)
+        self.core = lax.rem(self.shard, 2)
+        along_x = self.rank + 1 - 2 * lax.rem(self.rank, 2)
+        along_y = self.rank + 2 - 4 * lax.div(self.rank, 2)
+        self.first = jnp.where(self.core == 0, along_x, along_y)
+        self.second = jnp.where(self.core == 0, along_y, along_x)
+        self.across = 3 - self.rank
+        self.sibling = self.shard + 1 - 2 * self.core
+
+    def at(self, rank=None, shard=None):
+        return (self.rank if rank is None else rank, self.shard if shard is None else shard)
+
+    def greet(self, plane=True, sibling=False, chain=False, ring=False):
+        barrier = pltpu.get_barrier_semaphore()
+        count = 0
+        targets = []
+        if plane:
+            targets += [self.at(rank=r) for r in (self.first, self.second, self.across)]
+        if sibling:
+            targets.append(self.at(shard=self.sibling))
+        if ring:
+            targets += [self.at(shard=self.hop(k)) for k in range(1, self.chips)]
+        for target in targets:
+            pl.semaphore_signal(barrier, inc=1, device_id=target, device_id_type=MESH)
+            count += 1
+        if chain:
+            for step, there in ((2, self.z < self.chips - 1), (-2, self.z > 0)):
+
+                @pl.when(there)
+                def greet_neighbour(step=step):
+                    pl.semaphore_signal(
+                        barrier,
+                        inc=1,
+                        device_id=self.at(shard=self.shard + step),
+                        device_id_type=MESH,
+                    )
+
+                count = count + there.astype(jnp.int32)
+        pl.semaphore_wait(barrier, count)
+
+    def hop(self, k):
+        return 2 * lax.rem(self.z + k, self.chips) + self.core
+
+
+def under(condition, action):
+    if condition is None:
+        action()
+    else:
+        pl.when(condition)(action)
+
+
+class Message:
+    def __init__(self, links, src, dst, target, sent=None, comes=None):
+        index = links.take()
+        self.copy = pltpu.make_async_remote_copy(
+            src_ref=src,
+            dst_ref=dst,
+            send_sem=links.send.at[index],
+            recv_sem=links.recv.at[index],
+            device_id=target,
+            device_id_type=MESH,
+        )
+        self.sent, self.comes = sent, comes
+        links.open.append(self)
+        under(sent, self.copy.start)
+
+    def arrive(self):
+        under(self.comes, self.copy.wait_recv)
+
+    def leave(self):
+        under(self.sent, self.copy.wait_send)
+
+
+class Near:
+    def __init__(self, links, src, dst, where):
+        self.copy = pltpu.make_async_copy(src, dst, links.near.at[links.used_near])
+        links.used_near += 1
+        self.where = where
+        self.waits = True
+        under(where, self.copy.start)
+
+    def arrive(self):
+        if self.waits:
+            under(self.where, self.copy.wait)
+        self.waits = False
+
+
+class Links:
+    def __init__(self, send, recv, near):
+        self.send, self.recv, self.near = send, recv, near
+        self.used = 0
+        self.used_near = 0
+        self.open = []
+        self.open_near = []
+
+    def take(self):
+        self.used += 1
+        return self.used - 1
+
+    def keep(self, src, dst, where=None):
+        copy = Near(self, src, dst, where)
+        self.open_near.append(copy)
+        return copy
+
+    def drain(self):
+        for copy in self.open_near:
+            copy.arrive()
+        for message in self.open:
+            message.leave()
+
+
+LINK_SCRATCH = [
+    pltpu.SemaphoreType.DMA((128,)),
+    pltpu.SemaphoreType.DMA((128,)),
+    pltpu.SemaphoreType.DMA((32,)),
+]
+
+
+class PlaneGather:
+    def __init__(self, place, links, src, dst, parts):
+        self.place, self.links, self.dst = place, links, dst
+        rows = src.shape[0] // parts
+        self.cuts = [pl.ds(k * rows, rows) for k in range(parts)]
+        links.keep(src, dst.at[place.rank])
+        self.first, self.second = [], []
+        for cut in self.cuts:
+            for side, target in ((self.first, place.first), (self.second, place.second)):
+                block = dst.at[place.rank, cut]
+                side.append(Message(links, src.at[cut], block, place.at(rank=target)))
+        self.passed = []
+
+    def relay(self, k):
+        self.first[k].arrive()
+        block = self.dst.at[self.place.first, self.cuts[k]]
+        target = self.place.at(rank=self.place.second)
+        self.passed.append(Message(self.links, block, block, target))
+
+    def finish(self):
+        for message in self.second + self.passed:
+            message.arrive()
+
+
+class PlaneScatter:
+    def __init__(self, place, links, partial, landing, turn):
+        self.place, self.links, self.partial, self.landing, self.turn = (
+            place,
+            links,
+            partial,
+            landing,
+            turn,
+        )
+        target = place.at(rank=place.first)
+        self.far = Message(links, partial.at[place.across], landing.at[0], target)
+        self.near = Message(links, partial.at[place.first], landing.at[1], target)
+
+    def relay(self):
+        self.far.arrive()
+        mine = self.partial[self.place.second].astype(jnp.float32)
+        self.turn[...] = (mine + self.landing[0].astype(jnp.float32)).astype(jnp.bfloat16)
+        self.last = Message(
+            self.links, self.turn, self.landing.at[2], self.place.at(rank=self.place.second)
+        )
+
+    def total(self):
+        self.near.arrive()
+        self.last.arrive()
+        total = self.partial[self.place.rank].astype(jnp.float32)
+        return total + self.landing[1].astype(jnp.float32) + self.landing[2].astype(jnp.float32)
+
+
+class Chain:
+    def __init__(self, place, links, src, slot):
+        self.place, self.links, self.slot = place, links, slot
+        z, last = place.z, place.chips - 1
+        own = slot(place.shard)
+        self.up = Message(links, src, own, place.at(shard=place.shard + 2), z < last, z > 0)
+        self.down = Message(links, src, own, place.at(shard=place.shard - 2), z > 0, z < last)
+        self.beside = [Message(links, src, own, place.at(shard=place.sibling))]
+
+    def step(self, s):
+        place, links = self.place, self.links
+        z, last = place.z, place.chips - 1
+        below = self.slot(jnp.maximum(place.shard - 2 * s, place.core))
+        above = self.slot(jnp.minimum(place.shard + 2 * s, 2 * last + place.core))
+        self.up.arrive()
+        has_below, has_above = z >= s, z <= last - s
+        up = down = None
+        if s < last:
+            target = place.at(shard=place.shard + 2)
+            up = Message(links, below, below, target, has_below & (z < last), z >= s + 1)
+        self.beside.append(
+            Message(links, below, below, place.at(shard=place.sibling), has_below, has_below)
+        )
+        self.down.arrive()
+        if s < last:
+            target = place.at(shard=place.shard - 2)
+            down = Message(links, above, above, target, has_above & (z > 0), z <= last - s - 1)
+        self.beside.append(
+            Message(links, above, above, place.at(shard=place.sibling), has_above, has_above)
+        )
+        self.up, self.down = up, down
+
+    def finish(self):
+        for message in self.beside:
+            message.arrive()
+
+
+class Collect:
+    def __init__(self, place, links, part, own, other, landing):
+        self.place, self.links = place, links
+        self.own, self.other, self.landing = own, other, landing
+        self.beside = Message(
+            links, part.at[:, :, 1 - place.core], other, place.at(shard=place.sibling)
+        )
+        self.mine = links.keep(part.at[:, :, place.core], own)
+
+    def send(self):
+        self.mine.arrive()
+        self.beside.arrive()
+
+        def add(k, carry):
+            total = self.own[:, k].astype(jnp.float32) + self.other[:, k].astype(jnp.float32)
+            self.own[:, k] = total.astype(self.own.dtype)
+            return carry
+
+        place = self.place
+        lax.fori_loop(0, place.chips, add, 0)
+        self.along = []
+        for k in range(1, place.chips):
+            there = lax.rem(place.z + k, place.chips)
+            self.along.append(
+                Message(
+                    self.links,
+                    self.own.at[:, there],
+                    self.landing.at[k - 1],
+                    place.at(shard=place.hop(k)),
+                )
+            )
+
+    def total(self):
+        total = self.own[:, self.place.z].astype(jnp.float32)
+        for k, message in enumerate(self.along):
+            message.arrive()
+            total = total + self.landing[k].astype(jnp.float32)
+        return total
+
+
+def collect_scratch(lead, chips, rows, columns, dtype):
+    return [
+        pltpu.VMEM((lead, chips, rows, columns), dtype),
+        pltpu.VMEM((lead, chips, rows, columns), dtype),
+        pltpu.VMEM((chips - 1, lead, rows, columns), dtype),
+    ]
+
+
+class Deal:
+    def __init__(self, place, links, pairs):
+        self.messages = []
+        for part, dst in pairs:
+            self.messages.append(links.keep(part(place.rank), dst))
+            for rank in (place.first, place.second, place.across):
+                self.messages.append(Message(links, part(rank), dst, place.at(rank=rank)))
+
+    def arrive(self):
+        for message in self.messages:
+            message.arrive()
+
+
+def gather_kernel(
+    chips,
+    tokens,
+    suffix,
+    small,
+    w_query,
+    w_key,
+    w_value,
+    w_out,
+    w_up,
+    w_down,
+    all_tokens,
+    incoming,
+    all_small,
+    all_qkv,
+    all_out,
+    all_up,
+    all_down,
+    send,
+    recv,
+    near,
+):
+    place = Place(chips)
+    links = Links(send, recv, near)
+    place.greet(plane=True, sibling=True, chain=True)
+    rank, shard = place.rank, place.shard
+
+    def columns(weight, width):
+        return lambda r: weight.at[:, pl.ds(pl.multiple_of(r * width, 128), width)]
+
+    head_cols = w_query.shape[1] // 4
+    own_qkv = all_qkv.at[rank, shard]
+    pairs = [(lambda r: small, all_small.at[rank, shard])]
+    for i, weight in enumerate((w_query, w_key, w_value)):
+        own = own_qkv.at[:, pl.ds(i * head_cols, head_cols)]
+        pairs.append((columns(weight, head_cols), own))
+    deal_qkv = Deal(place, links, pairs)
+    gather = PlaneGather(place, links, tokens, all_tokens, 2)
+    deal_up = Deal(place, links, [(columns(w_up, w_up.shape[1] // 4), all_up.at[rank, shard])])
+
+    links.keep(w_out, all_out.at[shard])
+    links.keep(w_down, all_down.at[shard])
+    chain_out = Chain(place, links, w_out, lambda f: all_out.at[f])
+    deal_qkv.arrive()
+    small_slot = lambda f: all_small.at[:, f]
+    qkv_slot = lambda f: all_qkv.at[:, f]
+    up_slot = lambda f: all_up.at[:, f]
+    chain_small = Chain(place, links, small_slot(shard), small_slot)
+    chain_qkv = Chain(place, links, qkv_slot(shard), qkv_slot)
+    gather.relay(0)
+    gather.relay(1)
+    deal_up.arrive()
+    chain_up = Chain(place, links, up_slot(shard), up_slot)
+    chain_down = Chain(place, links, w_down, lambda f: all_down.at[f])
+
+    links.keep(suffix.at[block_of(rank)], incoming.at[0, rank])
+    links.keep(suffix.at[1], incoming.at[1, rank], rank == 0)
+    dealt = []
+    for r in (place.first, place.second, place.across):
+        dealt.append(
+            Message(links, suffix.at[block_of(r)], incoming.at[0, rank], place.at(rank=r))
+        )
+        dealt.append(
+            Message(links, suffix.at[1], incoming.at[1, rank], place.at(rank=r), r == 0, rank == 0)
+        )
+    for chain in (chain_out, chain_small, chain_qkv, chain_up, chain_down):
+        for s in range(1, chips):
+            chain.step(s)
+        chain.finish()
+    gather.finish()
+    for message in dealt:
+        message.arrive()
+    links.drain()
+
+
+def block_of(r):
+    return jnp.where(r == 0, 0, jnp.minimum(r + 1, GRAN - 1))
+
+
+def scatter_kernel(chips, partial, total, landing, turn, send, recv, near):
+    place = Place(chips)
+    links = Links(send, recv, near)
+    place.greet(plane=True)
+    scatter = PlaneScatter(place, links, partial, landing, turn)
+    scatter.relay()
+    total[...] = scatter.total()
+    links.drain()
+
+
+def spread_kernel(chips, block, blocks, send, recv, near):
+    place = Place(chips)
+    links = Links(send, recv, near)
+    place.greet(plane=True)
+    gather = PlaneGather(place, links, block, blocks, 2)
+    gather.relay(0)
+    gather.relay(1)
+    gather.finish()
+    links.drain()
+
+
+def middle_kernel(
+    chips,
+    branch,
+    terms,
+    part_down,
+    part_up,
+    all_branch,
+    term_in,
+    extra_in,
+    sum_down,
+    sum_up,
+    *scratch,
+):
+    own_down, other_down, land_down, own_up, other_up, land_up, turn, send, recv, near = scratch
+    place = Place(chips)
+    links = Links(send, recv, near)
+    place.greet(plane=True, sibling=True, ring=True)
+    rank = place.rank
+    collect_down = Collect(place, links, part_down, own_down, other_down, land_down)
+    collect_up = Collect(place, links, part_up, own_up, other_up, land_up)
+    gather = PlaneGather(place, links, branch, all_branch, 2)
+    collect_down.send()
+    collect_up.send()
+    gather.relay(0)
+    gather.relay(1)
+    links.keep(terms.at[0, rank], term_in.at[rank])
+    links.keep(terms.at[1, rank], extra_in, rank == 0)
+    dealt = []
+    for r in (place.first, place.second, place.across):
+        dealt.append(Message(links, terms.at[0, r], term_in.at[rank], place.at(rank=r)))
+        dealt.append(
+            Message(links, terms.at[1, r], extra_in, place.at(rank=r), rank == 0, r == 0)
+        )
+    sum_down[...] = collect_down.total()[0]
+    turn[...] = collect_up.total().astype(jnp.bfloat16)
+    deal_up = Deal(
+        place, links, [(lambda r: turn.at[r], sum_up.at[rank])]
+    )
+    gather.finish()
+    for message in dealt:
+        message.arrive()
+    deal_up.arrive()
+    links.drain()
+
+
+def last_kernel(
+    chips,
+    partial,
+    part_out,
+    part_qkv,
+    part_small,
+    total,
+    sum_out,
+    sum_qkv,
+    sum_small,
+    *scratch,
+):
+    landing, passing = scratch[:2]
+    own_out, other_out, land_out, own_qkv, other_qkv, land_qkv = scratch[2:8]
+    own_small, other_small, land_small, turn, turn_small, land_sums = scratch[8:14]
+    send, recv, near = scratch[14:]
+    place = Place(chips)
+    links = Links(send, recv, near)
+    place.greet(plane=True, sibling=True, ring=True)
+    rank = place.rank
+    collect_small = Collect(place, links, part_small, own_small, other_small, land_small)
+    collect_qkv = Collect(place, links, part_qkv, own_qkv, other_qkv, land_qkv)
+    collect_out = Collect(place, links, part_out, own_out, other_out, land_out)
+    scatter = PlaneScatter(place, links, partial, landing, passing)
+    collect_small.send()
+    collect_qkv.send()
+    collect_out.send()
+    scatter.relay()
+    turn_small[...] = collect_small.total()
+    deal_small = Deal(place, links, [(lambda r: turn_small.at[r], land_sums.at[rank])])
+    turn[...] = collect_qkv.total().astype(jnp.bfloat16)
+    deal_qkv = Deal(place, links, [(lambda r: turn.at[r], sum_qkv.at[rank])])
+    sum_out[...] = collect_out.total()[0]
+    total[...] = scatter.total()
+    deal_small.arrive()
+    sum_small[...] = land_sums[0] + land_sums[1] + land_sums[2] + land_sums[3]
+    deal_qkv.arrive()
+    links.drain()
+
+
+ANY = pl.BlockSpec(memory_space=pl.ANY)
+ON_CORE = pl.BlockSpec(memory_space=pltpu.VMEM)
+
+
+def connected(kernel, number, outs, out_specs, in_specs, scratch, operands):
+    return pl.pallas_call(
+        kernel,
+        out_shape=outs,
+        in_specs=in_specs,
+        out_specs=out_specs,
+        scratch_shapes=scratch + LINK_SCRATCH,
+        compiler_params=pltpu.CompilerParams(
+            collective_id=number, has_side_effects=True, vmem_limit_bytes=60 * 2**20
+        ),
+    )(*operands)
+
+
+def array(shape, dtype=jnp.bfloat16):
+    return jax.ShapeDtypeStruct(shape, dtype)
 
 
 def local_split(ranks, shards, *arguments):
+    chips = shards // 2
     (
         tokens,
         cotangent,
@@ -467,33 +941,44 @@
     scaling = HEAD_DIM ** (-0.5)
     rank = lax.axis_index("dp")
 
+    grads_out = cotangent.reshape(GRAN, tok_rows, model_width).astype(jnp.float32)
+    suffix = [grads_out[GRAN - 1]]
+    for level_idx in range(GRAN - 2, -1, -1):
+        suffix.insert(0, suffix[0] + grads_out[level_idx])
+    grad_hidden = suffix[0]
+    suffix = jnp.stack([s.astype(jnp.bfloat16) for s in suffix])
+
     small = jnp.concatenate([norm1_gain, norm1_bias, norm2_gain, norm2_bias, down_bias, up_bias])
-    small = lax.all_gather(small, ("dp", "fsdp"), axis=0, tiled=False).astype(jnp.float32)
+    small = jnp.pad(small, (0, 16 * 128 - small.shape[0])).reshape(16, 128)
+    own_tokens = tokens.reshape(tok_rows, model_width)
+    all_tokens, incoming, all_small, w_qkv, w_out, w_up, w_down = connected(
+        functools.partial(gather_kernel, chips),
+        1,
+        (
+            array((ranks, tok_rows, model_width)),
+            array((2, ranks, tok_rows, model_width)),
+            array((ranks, shards, 16, 128)),
+            array((ranks, shards, own, 3 * head_cols)),
+            array((shards, own, model_width)),
+            array((ranks, shards, own, ff_cols)),
+            array((shards, down_weight.shape[0], model_width)),
+        ),
+        [ANY] * 7,
+        [ANY] * 9,
+        [],
+        (own_tokens, suffix, small, query_weight, key_weight, value_weight, out_weight, up_weight, down_weight),
+    )
+    small = all_small.reshape(ranks * shards, 16 * 128)[:, : 5 * own + ff_cols // shards].astype(jnp.float32)
     gain_one, bias_one, gain_two, bias_two, b_down = (
         small[:, i * own : (i + 1) * own].reshape(model_width) for i in range(5)
     )
     b_up_all = small[:, 5 * own :].reshape(ranks, ff_cols)
     b_up = lax.dynamic_index_in_dim(b_up_all, rank, 0, keepdims=False)
-
-    def to_parts(weight):
-        return weight.reshape(own, ranks, -1).transpose(1, 0, 2)
-
-    mixed_weights = jnp.concatenate(
-        [to_parts(w) for w in (query_weight, key_weight, value_weight)], axis=2
-    )
-
-    def spread(parts):
-        parts = lax.all_to_all(parts, "dp", split_axis=0, concat_axis=0)
-        parts = lax.all_gather(parts, "fsdp", axis=1, tiled=False)
-        return parts.reshape(model_width, -1)
-
-    w_qkv = spread(mixed_weights)
-    w_out = lax.all_gather(out_weight, "fsdp", axis=0, tiled=True)
-    w_up = spread(to_parts(up_weight))
-    w_down = lax.all_gather(down_weight, "fsdp", axis=0, tiled=True)
-
-    own_tokens = tokens.reshape(tok_rows, model_width)
-    all_tokens = lax.all_gather(own_tokens, "dp", axis=0, tiled=True).astype(jnp.float32)
+    w_qkv = w_qkv.reshape(model_width, 3 * head_cols)
+    w_up = w_up.reshape(model_width, ff_cols)
+    w_out = w_out.reshape(head_cols, model_width)
+    w_down = w_down.reshape(ff_cols, model_width)
+    all_tokens = all_tokens.reshape(seq_len, model_width).astype(jnp.float32)
     normed_all, unused = norm_parts(all_tokens)
     attn_in = (normed_all * gain_one + bias_one).astype(jnp.bfloat16)
     qkv = product(attn_in, w_qkv)
@@ -520,89 +1005,98 @@
     )
     mixed_low = mixed.reshape(seq_len, head_cols).astype(jnp.bfloat16)
 
-    def add_up(partial):
-        return lax.psum_scatter(
-            partial.astype(jnp.bfloat16), "dp", scatter_dimension=0, tiled=True
-        ).astype(jnp.float32)
+    blocks_low = array((ranks, tok_rows, model_width))
+
+    def add_up(number, partial):
+        return connected(
+            functools.partial(scatter_kernel, chips),
+            number,
+            array((tok_rows, model_width), jnp.float32),
+            ON_CORE,
+            [ON_CORE],
+            [
+                pltpu.VMEM((3, tok_rows, model_width), jnp.bfloat16),
+                pltpu.VMEM((tok_rows, model_width), jnp.bfloat16),
+            ],
+            (partial.astype(jnp.bfloat16).reshape(ranks, tok_rows, model_width),),
+        )
 
     inputs = own_tokens.astype(jnp.float32)
-    hidden = inputs + add_up(product(mixed_low, w_out))
+    hidden = inputs + add_up(2, product(mixed_low, w_out))
     normed_two, inverse_two = norm_parts(hidden)
     ffn_in_own = (normed_two * gain_two + bias_two).astype(jnp.bfloat16)
-    ffn_in = lax.all_gather(ffn_in_own, "dp", axis=0, tiled=True)
+    ffn_in = connected(
+        functools.partial(spread_kernel, chips), 3, blocks_low, ANY, [ANY], [], (ffn_in_own,)
+    ).reshape(seq_len, model_width)
     preact = product(ffn_in, w_up) + b_up
     gated = gelu_value(preact).astype(jnp.bfloat16)
 
-    blocks, width = piece_blocks(ranks)
-    pieces = len(blocks[0])
+    half = ff_cols // 2
+    low_term = product(gated[:, :half], w_down[:half])
+    high_term = product(gated[:, half:], w_down[half:])
     terms = jnp.stack(
         [
-            product(gated[:, i * width : (i + 1) * width], w_down[i * width : (i + 1) * width])
-            .astype(jnp.bfloat16)
-            .reshape(ranks, tok_rows, model_width)
-            for i in range(pieces)
-        ],
-        axis=1,
-    )
-    terms = lax.all_to_all(terms, "dp", split_axis=0, concat_axis=0)
-    total = hidden + b_down
-    result_list = []
-    for level_idx in range(GRAN):
-        for source in range(ranks):
-            for i in range(pieces):
-                if blocks[source][i] == level_idx:
-                    total = total + terms[source, i].astype(jnp.float32)
-        result_list.append(total.astype(jnp.bfloat16))
-    activations = jnp.stack(result_list).reshape(GRAN, 1, tok_rows, model_width)
-
-    grads_out = cotangent.reshape(GRAN, tok_rows, model_width).astype(jnp.float32)
-    suffix = [grads_out[GRAN - 1]]
-    for level_idx in range(GRAN - 2, -1, -1):
-        suffix.insert(0, suffix[0] + grads_out[level_idx])
-    grad_hidden = suffix[0]
-    suffix = [s.astype(jnp.bfloat16) for s in suffix]
-    outgoing = jnp.stack([jnp.stack([suffix[b] for b in blocks[j]]) for j in range(ranks)])
-    incoming = lax.all_to_all(outgoing, "dp", split_axis=0, concat_axis=0)
-    incoming = incoming.transpose(1, 0, 2, 3).reshape(pieces, seq_len, model_width)
-
+            (low_term + jnp.where(rank == 0, 0.0, high_term)).astype(jnp.bfloat16),
+            high_term.astype(jnp.bfloat16),
+        ]
+    ).reshape(2, ranks, tok_rows, model_width)
+    split_grads = [
+        incoming[0].reshape(seq_len, model_width),
+        jnp.where(rank == 0, incoming[1], incoming[0]).reshape(seq_len, model_width),
+    ]
     grad_gated = jnp.concatenate(
-        [back_product(incoming[i], w_down[i * width : (i + 1) * width]) for i in range(pieces)],
+        [back_product(split_grads[i], w_down[i * half : (i + 1) * half]) for i in range(2)],
         axis=1,
     )
     grad_pre_wide = grad_gated * gelu_grad(preact)
     grad_pre = grad_pre_wide.astype(jnp.bfloat16)
     grad_up_bias = jnp.sum(grad_pre_wide, axis=0)
-    grad_ffn_in = add_up(back_product(grad_pre, w_up))
-
-    def collect(grad):
-        return lax.psum_scatter(
-            grad.astype(jnp.bfloat16), "fsdp", scatter_dimension=0, tiled=True
-        )
-
-    def collect_columns(grad):
-        columns = grad.shape[1]
-        grad = grad.astype(jnp.bfloat16).reshape(ranks, shards, own, columns)
-        grad = grad.transpose(1, 0, 2, 3).reshape(model_width, columns)
-        grad = lax.psum_scatter(grad, "fsdp", scatter_dimension=0, tiled=True)
-        grad = grad.reshape(ranks, own, columns)
-        grad = lax.all_to_all(grad, "dp", split_axis=0, concat_axis=0)
-        return grad.astype(jnp.float32)
-
-    sum_down = collect(
-        jnp.concatenate(
-            [gram_product(gated[:, i * width : (i + 1) * width], incoming[i]) for i in range(pieces)],
-            axis=0,
-        )
-    ).astype(jnp.float32)
-    sum_up = collect_columns(gram_product(ffn_in, grad_pre))
-    sum_up = sum_up.transpose(1, 0, 2).reshape(own, FF)
-
+    grad_ffn_in = add_up(4, back_product(grad_pre, w_up))
+
+    part_down = jnp.concatenate(
+        [gram_product(gated[:, i * half : (i + 1) * half], split_grads[i]) for i in range(2)],
+        axis=0,
+    ).astype(jnp.bfloat16)
+    part_up = gram_product(ffn_in, grad_pre).astype(jnp.bfloat16)
     grad_down_bias = jnp.sum(grad_hidden, axis=0)
     grad_gain_two = jnp.sum(grad_ffn_in * normed_two, axis=0)
     grad_bias_two = jnp.sum(grad_ffn_in, axis=0)
     grad_hidden = grad_hidden + norm_backward(grad_ffn_in, normed_two, inverse_two, gain_two)
-    grad_branch = lax.all_gather(grad_hidden.astype(jnp.bfloat16), "dp", axis=0, tiled=True)
-    sum_out = collect(gram_product(mixed_low, grad_branch)).astype(jnp.float32)
+    down_rows = ff_cols // shards
+    grad_branch, term_in, extra_in, sum_down, sum_up = connected(
+        functools.partial(middle_kernel, chips),
+        5,
+        (
+            blocks_low,
+            blocks_low,
+            array((tok_rows, model_width)),
+            array((down_rows, model_width), jnp.float32),
+            array((ranks, own, ff_cols)),
+        ),
+        [ANY, ANY, ANY, ON_CORE, ANY],
+        [ANY] * 4,
+        collect_scratch(1, chips, down_rows, model_width, jnp.bfloat16)
+        + collect_scratch(ranks, chips, own, ff_cols, jnp.bfloat16)
+        + [pltpu.VMEM((ranks, own, ff_cols), jnp.bfloat16)],
+        (
+            grad_hidden.astype(jnp.bfloat16),
+            terms,
+            part_down.reshape(1, chips, 2, down_rows, model_width),
+            part_up.reshape(ranks, chips, 2, own, ff_cols),
+        ),
+    )
+    grad_branch = grad_branch.reshape(seq_len, model_width)
+    sum_up = sum_up.astype(jnp.float32).transpose(1, 0, 2).reshape(own, FF)
+    total = hidden + b_down + term_in[0].astype(jnp.float32)
+    result_list = [total.astype(jnp.bfloat16)]
+    total = total + extra_in.astype(jnp.float32)
+    result_list.append(total.astype(jnp.bfloat16))
+    total = total + term_in[1].astype(jnp.float32)
+    result_list.append(total.astype(jnp.bfloat16))
+    total = total + term_in[2].astype(jnp.float32) + term_in[3].astype(jnp.float32)
+    result_list.append(total.astype(jnp.bfloat16))
+    activations = jnp.stack(result_list).reshape(GRAN, 1, tok_rows, model_width)
+    part_out = gram_product(mixed_low, grad_branch).astype(jnp.bfloat16)
     grad_mixed = (
         back_product(grad_branch, w_out).astype(jnp.bfloat16).reshape(seq_len, heads, HEAD_DIM)
     )
@@ -627,40 +1121,80 @@
         ],
         axis=1,
     ).astype(jnp.bfloat16)
-    sum_qkv = collect_columns(gram_product(attn_in, grad_qkv)).transpose(1, 0, 2)
+    part_qkv = gram_product(attn_in, grad_qkv).astype(jnp.bfloat16)
+    partial = back_product(grad_qkv, w_qkv).astype(jnp.bfloat16)
+    sums = jnp.stack([grad_gain_two, grad_bias_two, grad_down_bias])
+    sums = sums.reshape(3, ranks, shards, own).transpose(1, 2, 0, 3).reshape(ranks, shards, 3 * own)
+    here = (jnp.arange(ranks) == rank).astype(jnp.float32)[:, None, None]
+    sums = jnp.concatenate([sums, here * grad_up_bias.reshape(1, shards, -1)], axis=2)
+    used = sums.shape[2]
+    sums = jnp.pad(sums, ((0, 0), (0, 0), (0, 1024 - used)))
+    grad_attn_in, sum_out, sum_qkv, sums = connected(
+        functools.partial(last_kernel, chips),
+        6,
+        (
+            array((tok_rows, model_width), jnp.float32),
+            array((own, model_width), jnp.float32),
+            array((ranks, own, 3 * head_cols)),
+            array((8, 128), jnp.float32),
+        ),
+        [ON_CORE, ON_CORE, ANY, ON_CORE],
+        [ON_CORE, ANY, ANY, ANY],
+        [
+            pltpu.VMEM((3, tok_rows, model_width), jnp.bfloat16),
+            pltpu.VMEM((tok_rows, model_width), jnp.bfloat16),
+        ]
+        + collect_scratch(1, chips, own, model_width, jnp.bfloat16)
+        + collect_scratch(ranks, chips, own, 3 * head_cols, jnp.bfloat16)
+        + collect_scratch(ranks, chips, 8, 128, jnp.float32)
+        + [
+            pltpu.VMEM((ranks, own, 3 * head_cols), jnp.bfloat16),
+            pltpu.VMEM((ranks, 8, 128), jnp.float32),
+            pltpu.VMEM((ranks, 8, 128), jnp.float32),
+        ],
+        (
+            partial.reshape(ranks, tok_rows, model_width),
+            part_out.reshape(1, chips, 2, own, model_width),
+            part_qkv.reshape(ranks, chips, 2, own, 3 * head_cols),
+            sums.reshape(ranks, chips, 2, 8, 128),
+        ),
+    )
+    sums = sums.reshape(1024)
+    sum_gain_two, sum_bias_two, sum_down_bias = (sums[i * own : (i + 1) * own] for i in range(3))
+    sum_up_bias = sums[3 * own : used]
+    sum_qkv = sum_qkv.astype(jnp.float32).transpose(1, 0, 2)
     sum_query, sum_key, sum_value = (
         sum_qkv[:, :, i * head_cols : (i + 1) * head_cols].reshape(own, model_width)
         for i in range(3)
     )
-    grad_attn_in = add_up(back_product(grad_qkv, w_qkv))
     normed_one, inverse_one = norm_parts(inputs)
     grad_gain_one = jnp.sum(grad_attn_in * normed_one, axis=0)
     grad_bias_one = jnp.sum(grad_attn_in, axis=0)
     grad_inputs = grad_hidden + norm_backward(grad_attn_in, normed_one, inverse_one, gain_one)
 
-    sums = jnp.stack([grad_gain_one, grad_bias_one, grad_gain_two, grad_bias_two, grad_down_bias])
-    sums = lax.psum_scatter(
-        sums.reshape(5, ranks * shards, own).transpose(1, 0, 2).reshape(ranks * shards, 5 * own),
+    sums_one = lax.psum_scatter(
+        jnp.concatenate(
+            [g.reshape(ranks * shards, own) for g in (grad_gain_one, grad_bias_one)], axis=1
+        ),
         ("dp", "fsdp"),
         scatter_dimension=0,
         tiled=True,
-    ).reshape(5, own)
-    sum_up_bias = lax.psum_scatter(grad_up_bias, "fsdp", scatter_dimension=0, tiled=True)
+    ).reshape(2, own)
     return (
         activations,
         grad_inputs.astype(jnp.bfloat16).reshape(1, tok_rows, model_width),
-        sums[0],
-        sums[1],
+        sums_one[0],
+        sums_one[1],
         sum_query,
         sum_key,
         sum_value,
         sum_out,
-        sums[2],
-        sums[3],
+        sum_gain_two,
+        sum_bias_two,
         sum_up,
         sum_up_bias,
         sum_down,
-        sums[4],
+        sum_down_bias,
     )
 
 
@@ -683,7 +1217,7 @@
     )
     ranks, shards = mesh.shape["dp"], mesh.shape["fsdp"]
     local = local_gathered
-    if HEADS % ranks == 0:
+    if ranks == 4 and shards % 2 == 0:
         local = functools.partial(local_split, ranks, shards)
     return jax.shard_map(
         local,

time: 877 us -> 696 us (0.79)
  waiting for transfers between devices: 448 us -> 0 us
  Pallas kernels: 0 us -> 432 us
  blocking collectives: 129 us -> 42.1 us
  starting transfers between devices: 20.3 us -> 0 us
  local copies, waits for them, and re-layouts: 67.6 us -> 47.7 us
  between operations: 16 us -> 1.69 us
  other arithmetic: 64.7 us -> 53.9 us
    pallas_call x0 -> x6, Pallas kernels: none -> 432 us  [connected(): pl.pallas_call(kernel, out_shape=outs, in_specs=in_specs, out_specs=out_s...]
    reduce_scatter x7 -> x0, waiting for transfers between devices: 268 us -> none  [the longest x3 170 us: add_up(): lax.psum_scatter(partial.astype(jnp.bfloat16), 'dp', scatter_dimension=0,...]
    all_gather x7 -> x0, waiting for transfers between devices: 151 us -> none  [the longest x2 66.9 us: spread(): parts = lax.all_gather(parts, 'fsdp', axis=1, tiled=False)]
    unnamed x3 -> x1, blocking collectives: 96.3 us -> 42.1 us
    all_to_all x2 -> x0, blocking collectives: 32.8 us -> none  [spread(): parts = lax.all_to_all(parts, 'dp', split_axis=0, concat_axis=0)]
    all_to_all x4 -> x0, waiting for transfers between devices: 26.5 us -> none  [the longest x1 18 us: local_split(): incoming = lax.all_to_all(outgoing, 'dp', split_axis=0, concat_axis=0)]
    all_to_all x4 -> x0, starting transfers between devices: 18.4 us -> none  [the longest x2 7.79 us: collect_columns(): grad = lax.all_to_all(grad, 'dp', split_axis=0, concat_axis=0)]
    reshape x8 -> x5, local copies, waits for them, and re-layouts: 11.4 us -> 1.94 us  [the longest x1 1.11 us: local_split(): sum_up = sum_up.astype(jnp.float32).transpose(1, 0, 2).reshape(own, FF)]
  transfers between devices with their start and end apart: 18 -> 0, of which waited for: 13 -> 0; matrix products, arithmetic and copies ran while one was open for 24% -> 0% of each run, Pallas kernels for 0% -> 0%
where the time goes in v2:
time: 696 us; the launch traced here: 690 us
  Pallas kernels  432 us (62%)
  matrix products  113 us (16%)
  other arithmetic  53.9 us (8%)
  local copies, waits for them, and re-layouts  47.7 us (7%)
  blocking collectives  42.1 us (6%)
    pallas_call x6, Pallas kernels, connected(): pl.pallas_call(kernel, out_shape=outs, in_specs=in_specs, out_specs=out_s...  432 us
    unnamed x1, blocking collectives  42.1 us
    dot_general x5, matrix products, product(): return jnp.dot(left, right, preferred_element_type=jnp.float32)  29.6 us
    dot_general x5, matrix products, back_product(): lax.dot_general(left, right, (((1,), (1,)), ((), ())), preferred_element_...  28 us
    dot_general x5, matrix products, gram_product(): lax.dot_general(left, right, (((0,), (0,)), ((), ())), preferred_element_...  26.9 us
    unnamed x122, local copies, waits for them, and re-layouts  19.8 us

profile of v2, /device:TPU:0, one launch (start us, length us, event | category | flops | bytes accessed | tf_op | source)
XLA Modules:
  0.0 689.9 jit_solution(803486608517065711)
XLA Ops:
  0.7 4.3 concatenate.37
  17.3 150.2 %shard_map.245 = (bf16[4,256,1536]{2,1,0:T(8,128)(2,1)}, bf16[2,4,256,1536]{3,2,1,0:T(8,128)(2,1)}, bf16[4,8,16,128]{3,2,1,0:T(8,128)(2,1)}, bf16[4,8,48,1152]{3...) custom-call(bf16[256,1536]{1,0:T(8,128)(2,1)} %bitcast.186, ...), custom_call_target="tpu_custom_call" | custom-call | tf_op jit(solution)/shard_map/pallas_call | solution.py:900
  177.6 4.2 fusion.65
  206.1 4.0 fusion.58
  214.4 4.3 fusion.67
  218.7 4.3 fusion.66
  225.6 4.3 exponential_reduce_fusion
  230.2 5.7 bitcast_convert_fusion
  239.4 34.4 %shard_map.246 = f32[256,1536]{1,0:T(8,128)} custom-call(bf16[4,256,1536]{2,1,0:T(8,128)(2,1)} %bitcast.198), custom_call_target="tpu_custom_call" | custom-call | tf_op jit(solution)/shard_map/pallas_call | solution.py:900
  277.3 32.0 %shard_map.247 = bf16[4,256,1536]{2,1,0:T(8,128)(2,1)} custom-call(bf16[256,1536]{1,0:T(8,128)(2,1)} %add_convert_fusion.4.block), custom_call_target="tpu_custom_call" | custom-call | tf_op jit(solution)/shard_map/pallas_call | solution.py:900
  309.3 15.7 %fusion.53 = (f32[1536]{0:T(1024)S(1)}, bf16[1024,1536]{0,1:T(8,128)(2,1)}, bf16[1024,1536]{0,1:T(8,128)(2,1)}) fusion(f32[1536]{0:T(1024)S(1)} %dynamic-slice_reduce_fusion, f32[1024,768]{0,1:T(8,128)} %fusion.67, f32[1024,768]{0,1:T(8,128)} %fusion.66, bf16[1024,1536]{1,0:T(8,128)(2,1)} %bitcast.199, bf16[1536,1536]{1,0:T(8,128)(2,1)} %bitcast.229), kind=kOutput, calls=%fused_computation.156 | convolution fusion | flops 4869585408 | bytes 20459520 | tf_op jit(solution)/shard_map/dot_general | solution.py:22
  325.1 5.5 convolution_convert_fusion.6
  334.5 6.8 convolution_convert_fusion.2
  341.3 34.1 %shard_map.248 = f32[256,1536]{1,0:T(8,128)} custom-call(bf16[4,256,1536]{2,1,0:T(8,128)(2,1)} %bitcast.197), custom_call_target="tpu_custom_call" | custom-call | tf_op jit(solution)/shard_map/pallas_call | solution.py:900
  375.4 5.0 pad_maximum_fusion.1
  385.0 9.4 %convolution_convert_fusion.1 = bf16[1536,1536]{1,0:T(8,128)(2,1)} fusion(bf16[1024,1536]{1,0:T(8,128)(2,1)} %bitcast.200, bf16[1024,1536]{0,1:T(8,128)(2,1)} %get-tuple-element.99), kind=kOutput, calls=%fused_computation.8 | convolution fusion | flops 4834197504 | bytes 11010048 | tf_op jit(solution)/shard_map/dot_general | solution.py:26
  403.7 109.7 %shard_map.249 = (bf16[4,256,1536]{2,1,0:T(8,128)(2,1)}, bf16[4,256,1536]{2,1,0:T(8,128)(2,1)}, bf16[256,1536]{1,0:T(8,128)(2,1)}, f32[192,1536]{1,0:T(8,128)}, bf16[4,48,1536]{2,1,0:T(8,128)(2,1)}) custom-call(bf16[256,1536]{1,0:T(8,128)(2,1)} %get-tuple-element.100.branch, bf16[2,4,256,1536]{3,2,1,0:T(8,128)(2,1)} %pad_maximum_fusion.terms, ...), custom_call_target="tpu_custom_call" | custom-call | tf_op jit(solution)/shard_map/pallas_call | solution.py:900
  525.3 4.3 convolution_convert_fusion.8
  529.6 8.0 %multiply_convert_fusion = bf16[3,1024,1024]{1,2,0:T(8,128)(2,1)} fusion(f32[3,1024,1024]{1,2,0:T(8,128)S(1)} %bitcast.185, f32[3,1024]{1,0:T(4,128)S(1)} %fusion.25, f32[3,1024]{1,0:T(4,128)S(1)} %log_add_fusion, pred[1024,1024]{0,1:T(8,128)(4,1)S(1)} %copy-done.4, bf16[1024,3,128]{0,2,1:T(8,128)(2,1)} %bitcast.219, bf16[1024,3,128]{0,2,1:T(8,128)(2,1)} %bitcast.212), kind=kOutput, calls=%fused_computation | convolution fusion | flops 821035008 | bytes 21520384 | tf_op jit(solution)/shard_map/qhd,khd->hqk/dot_general | solution.py:1105
  537.5 6.0 multiply_bitcast_fusion
  548.8 8.8 %convolution_convert_fusion.4 = bf16[1024,1536]{1,0:T(8,128)(2,1)} fusion(bf16[1536,1152]{1,0:T(8,128)(2,1)} %bitcast.233, bf16[1024,384]{0,1:T(8,128)(2,1)} %bitcast.241, bf16[1024,384]{0,1:T(8,128)(2,1)S(1)} %bitcast.215, bf16[1024,384]{0,1:T(8,128)(2,1)} %bitcast.213), kind=kOutput, calls=%fused_computation.30 | convolution fusion | flops 3632529408 | bytes 9043968 | tf_op jit(solution)/shard_map/dot_general | solution.py:32
  557.7 5.8 convolution_convert_fusion
  563.4 71.4 %shard_map.250 = (f32[256,1536]{1,0:T(8,128)}, f32[48,1536]{1,0:T(8,128)}, bf16[4,48,1152]{2,1,0:T(8,128)(2,1)}, f32[8,128]{1,0:T(8,128)}) custom-call(bf16[4,256,1536]{2,1,0:T(8,128)(2,1)} %bitcast.201, bf16[1,4,2,48,1536]{4,3,2,1,0:T(8,128)(2,1)} %bitcast.210, bf16[4,4,2,48,1152]{4,3,2,1,0:T(8,128)(2,1)} %bitcast.195, f32[4,4,2,8,128]{4,3,2,1,0:T(8,128)} %bitcast.220), custom_call_target="tpu_custom_call" | custom-call | tf_op jit(solution)/shard_map/pallas_call | solution.py:900
  641.6 42.1 %all-reduce.2 = f32[32,96]{1,0:T(8,128)S(1)} all-reduce(f32[32,96]{1,0:T(8,128)S(1)} %pad_maximum_fusion.11), channel_id=2, replica_groups=mesh['dp'=4,'fsdp'=8] {'dp','fsdp'}, use_global_device_ids=true, to_apply=%region_18.19.clone | all-reduce | flops 3072 | bytes 24576
  (216 shorter events, 107.9 us)
Async XLA Ops:
  0.6 10.7 %copy-start.22 = (bf16[4,1,256,1536]{3,2,1,0:T(8,128)(2,1)S(1)}, bf16[4,1,256,1536]{3,2,1,0:T(8,128)(2,1)}, u32[]{:S(2)}) copy-start(bf16[4,1,256,1536]{3,2,1,0:T(8,128)(2,1)} %param.15) | copy-start | bytes 9437188
  205.5 17.5 %copy-start.10 = (bf16[1024,3,64]{2,0,1:T(8,128)(2,1)}, bf16[1024,3,64]{2,0,1:T(8,128)(2,1)S(1)}, u32[]{:S(2)}) copy-start(bf16[1024,3,64]{2,0,1:T(8,128)(2,1)S(1)} %get-tuple-element.118) | copy-start | bytes 1179652
  205.5 17.5 %copy-start.11 = (bf16[1024,3,64]{2,0,1:T(8,128)(2,1)}, bf16[1024,3,64]{2,0,1:T(8,128)(2,1)S(1)}, u32[]{:S(2)}) copy-start(bf16[1024,3,64]{2,0,1:T(8,128)(2,1)S(1)} %get-tuple-element.119) | copy-start | bytes 1179652
  206.0 17.0 %copy-start.18 = (bf16[1024,3,128]{2,0,1:T(8,128)(2,1)}, bf16[1024,3,128]{2,0,1:T(8,128)(2,1)S(1)}, u32[]{:S(2)}) copy-start(bf16[1024,3,128]{2,0,1:T(8,128)(2,1)S(1)} %fusion.23) | copy-start | bytes 2359300
  210.1 8.7 %copy-start.24 = (bf16[4,192,1536]{2,1,0:T(8,128)(2,1)}, bf16[4,192,1536]{2,1,0:T(8,128)(2,1)S(1)}, u32[]{:S(2)}) copy-start(bf16[4,192,1536]{2,1,0:T(8,128)(2,1)S(1)} %get-tuple-element.114) | copy-start | bytes 7077892
  211.8 6.9 copy-start.8
  230.2 5.7 copy-start.41
  239.4 34.5 %copy-start.2 = (bf16[1,256,1536]{2,1,0:T(8,128)(2,1)S(1)}, bf16[1,256,1536]{2,1,0:T(8,128)(2,1)}, u32[]{:S(2)}) copy-start(bf16[1,256,1536]{2,1,0:T(8,128)(2,1)} %param.14) | copy-start | bytes 2359300
  309.3 15.7 %copy-start.9 = (bf16[1,4,256,1536]{3,2,1,0:T(8,128)(2,1)S(1)}, bf16[1,4,256,1536]{3,2,1,0:T(8,128)(2,1)}, u32[]{:S(2)}) copy-start(bf16[1,4,256,1536]{3,2,1,0:T(8,128)(2,1)} %copy-done.8) | copy-start | bytes 9437188
  325.1 9.4 %slice-start.5 = ((s8[4718592]{0:T(1024)(128)(4,1)}), s8[4194304]{0:T(1024)(128)(4,1)S(1)}, s32[]{:S(2)}) async-start(s8[4718592]{0:T(1024)(128)(4,1)} %bitcast.230), calls=%async_computation.5 | async-start | bytes 8388608
  385.0 9.4 %copy-start.27 = (bf16[4,192,1536]{2,1,0:T(8,128)(2,1)S(1)}, bf16[4,192,1536]{2,1,0:T(8,128)(2,1)}, u32[]{:S(2)}) copy-start(bf16[4,192,1536]{2,1,0:T(8,128)(2,1)} %copy-done.26) | copy-start | bytes 7077892
  385.0 9.4 %copy-start.46 = (bf16[1024,1536]{0,1:T(8,128)(2,1)S(1)}, bf16[1024,1536]{0,1:T(8,128)(2,1)}, u32[]{:S(2)}) copy-start(bf16[1024,1536]{0,1:T(8,128)(2,1)} %get-tuple-element.104) | copy-start | bytes 9437188
  517.2 7.0 %copy-start.33 = (bf16[1024,384]{0,1:T(8,128)(2,1)}, bf16[1024,384]{0,1:T(8,128)(2,1)S(1)}, u32[]{:S(2)}) copy-start(bf16[1024,384]{0,1:T(8,128)(2,1)S(1)} %convolution_convert_fusion.9) | copy-start | bytes 2359300
  517.5 6.7 slice-start
  517.5 6.7 slice-start.1
  537.5 6.0 copy-start.12
  537.5 6.1 copy-start.19
  548.8 8.9 %copy-start.21 = (bf16[1024,1536]{1,0:T(8,128)(2,1)S(1)}, bf16[1024,1536]{1,0:T(8,128)(2,1)}, u32[]{:S(2)}) copy-start(bf16[1024,1536]{1,0:T(8,128)(2,1)} %fusion.10) | copy-start | bytes 9437188
  548.8 8.8 %copy-start.32 = (bf16[1024,3,128]{0,2,1:T(8,128)(2,1)S(1)}, bf16[1024,3,128]{0,2,1:T(8,128)(2,1)}, u32[]{:S(2)}) copy-start(bf16[1024,3,128]{0,2,1:T(8,128)(2,1)} %copy.87) | copy-start | bytes 2359300
  548.8 8.8 %copy-start.44 = (bf16[3,128,1024]{2,1,0:T(8,128)(2,1)S(1)}, bf16[3,128,1024]{2,1,0:T(8,128)(2,1)}, u32[]{:S(2)}) copy-start(bf16[3,128,1024]{2,1,0:T(8,128)(2,1)} %convolution_convert_fusion.8) | copy-start | bytes 2359300
  563.4 74.3 %copy-start.38 = (f32[1536]{0:T(1024)S(1)}, f32[1536]{0:T(1024)}, u32[]{:S(2)}) copy-start(f32[1536]{0:T(1024)} %copy-done.37) | copy-start | bytes 18436
  563.4 76.5 %copy-start.16 = (f32[256,1536]{1,0:T(8,128)S(1)}, f32[256,1536]{1,0:T(8,128)}, u32[]{:S(2)}) copy-start(f32[256,1536]{1,0:T(8,128)} %get-tuple-element.101) | copy-start | bytes 4718596
  637.7 46.7 %copy-start.35 = (bf16[4,48,1152]{2,1,0:T(8,128)(2,1)S(1)}, bf16[4,48,1152]{2,1,0:T(8,128)(2,1)}, u32[]{:S(2)}) copy-start(bf16[4,48,1152]{2,1,0:T(8,128)(2,1)} %get-tuple-element.41) | copy-start | bytes 1327108
  641.4 45.3 %copy-start.34 = (bf16[4,48,1536]{2,1,0:T(8,128)(2,1)S(1)}, bf16[4,48,1536]{2,1,0:T(8,128)(2,1)}, u32[]{:S(2)}) copy-start(bf16[4,48,1536]{2,1,0:T(8,128)(2,1)} %get-tuple-element.44) | copy-start | bytes 1769476
  (31 other events, 119.4 us)

commit v3 on v2

--- a/solution.py
+++ b/solution.py
@@ -557,6 +557,24 @@
 ]
 
 
+def normed(values):
+    centred = values - jnp.mean(values, axis=-1, keepdims=True)
+    inverse = lax.rsqrt(jnp.mean(centred * centred, axis=-1, keepdims=True) + epsilon)
+    return centred * inverse, inverse
+
+
+def in_rows(count, step, body):
+    def one(i, carry):
+        body(pl.ds(pl.multiple_of(i * step, step), step))
+        return carry
+
+    lax.fori_loop(0, count // step, one, 0)
+
+
+def turn_half(values, cosine, sine):
+    return values * cosine + pltpu.roll(values, HEAD_DIM // 2, 1) * sine
+
+
 class PlaneGather:
     def __init__(self, place, links, src, dst, parts):
         self.place, self.links, self.dst = place, links, dst
@@ -590,23 +608,39 @@
             landing,
             turn,
         )
-        target = place.at(rank=place.first)
-        self.far = Message(links, partial.at[place.across], landing.at[0], target)
-        self.near = Message(links, partial.at[place.first], landing.at[1], target)
+        self.target = place.at(rank=place.first)
+
+    def send_far(self):
+        self.far = Message(
+            self.links, self.partial.at[self.place.across], self.landing.at[0], self.target
+        )
+
+    def send_near(self):
+        self.near = Message(
+            self.links, self.partial.at[self.place.first], self.landing.at[1], self.target
+        )
 
     def relay(self):
         self.far.arrive()
-        mine = self.partial[self.place.second].astype(jnp.float32)
-        self.turn[...] = (mine + self.landing[0].astype(jnp.float32)).astype(jnp.bfloat16)
+
+        def add(cut):
+            mine = self.partial[self.place.second, cut].astype(jnp.float32)
+            mine = mine + self.landing[0, cut].astype(jnp.float32)
+            self.turn[cut] = mine.astype(jnp.bfloat16)
+
+        in_rows(self.turn.shape[0], 64, add)
         self.last = Message(
             self.links, self.turn, self.landing.at[2], self.place.at(rank=self.place.second)
         )
 
-    def total(self):
+    def settle(self):
         self.near.arrive()
         self.last.arrive()
-        total = self.partial[self.place.rank].astype(jnp.float32)
-        return total + self.landing[1].astype(jnp.float32) + self.landing[2].astype(jnp.float32)
+
+    def total(self, cut):
+        total = self.partial[self.place.rank, cut].astype(jnp.float32)
+        total = total + self.landing[1, cut].astype(jnp.float32)
+        return total + self.landing[2, cut].astype(jnp.float32)
 
 
 class Chain:
@@ -646,52 +680,41 @@
             message.arrive()
 
 
-class Collect:
-    def __init__(self, place, links, part, own, other, landing):
-        self.place, self.links = place, links
-        self.own, self.other, self.landing = own, other, landing
-        self.beside = Message(
+class Beside:
+    def __init__(self, place, links, part, other):
+        self.place, self.part, self.other = place, part, other
+        self.message = Message(
             links, part.at[:, :, 1 - place.core], other, place.at(shard=place.sibling)
         )
-        self.mine = links.keep(part.at[:, :, place.core], own)
-
-    def send(self):
-        self.mine.arrive()
-        self.beside.arrive()
-
-        def add(k, carry):
-            total = self.own[:, k].astype(jnp.float32) + self.other[:, k].astype(jnp.float32)
-            self.own[:, k] = total.astype(self.own.dtype)
+
+    def add(self):
+        self.message.arrive()
+        core = self.place.core
+
+        def one(k, carry):
+            total = self.part[:, k, core].astype(jnp.float32) + self.other[:, k].astype(jnp.float32)
+            self.part[:, k, core] = total.astype(self.part.dtype)
             return carry
 
-        place = self.place
-        lax.fori_loop(0, place.chips, add, 0)
-        self.along = []
+        lax.fori_loop(0, self.place.chips, one, 0)
+
+
+class Along:
+    def __init__(self, place, links, share, landing):
+        self.landing = landing
+        self.messages = []
         for k in range(1, place.chips):
             there = lax.rem(place.z + k, place.chips)
-            self.along.append(
-                Message(
-                    self.links,
-                    self.own.at[:, there],
-                    self.landing.at[k - 1],
-                    place.at(shard=place.hop(k)),
-                )
+            self.messages.append(
+                Message(links, share(there), landing.at[k - 1], place.at(shard=place.hop(k)))
             )
 
-    def total(self):
-        total = self.own[:, self.place.z].astype(jnp.float32)
-        for k, message in enumerate(self.along):
+    def total(self, mine):
+        total = mine.astype(jnp.float32)
+        for k, message in enumerate(self.messages):
             message.arrive()
             total = total + self.landing[k].astype(jnp.float32)
         return total
-
-
-def collect_scratch(lead, chips, rows, columns, dtype):
-    return [
-        pltpu.VMEM((lead, chips, rows, columns), dtype),
-        pltpu.VMEM((lead, chips, rows, columns), dtype),
-        pltpu.VMEM((chips - 1, lead, rows, columns), dtype),
-    ]
 
 
 class Deal:
@@ -707,7 +730,11 @@
             message.arrive()
 
 
-def gather_kernel(
+def block_of(r):
+    return jnp.where(r == 0, 0, jnp.minimum(r + 1, GRAN - 1))
+
+
+def forward_kernel(
     chips,
     tokens,
     suffix,
@@ -718,13 +745,33 @@
     w_out,
     w_up,
     w_down,
+    comb,
+    mask,
+    cosine,
+    sine,
     all_tokens,
+    attn_in,
+    qkv_rot,
+    mixed_low,
+    hidden,
+    all_ffn_in,
+    gains,
     incoming,
-    all_small,
     all_qkv,
     all_out,
     all_up,
     all_down,
+    tokens_v,
+    attn_v,
+    rot_v,
+    mixed_v,
+    qkv_v,
+    out_v,
+    partial,
+    landing,
+    passing,
+    ffn_v,
+    all_small,
     send,
     recv,
     near,
@@ -733,35 +780,79 @@
     links = Links(send, recv, near)
     place.greet(plane=True, sibling=True, chain=True)
     rank, shard = place.rank, place.shard
+    ranks, tok_rows, model_width = tokens_v.shape
+    head_cols = w_query.shape[1] // ranks
+    heads = head_cols // HEAD_DIM
 
     def columns(weight, width):
         return lambda r: weight.at[:, pl.ds(pl.multiple_of(r * width, 128), width)]
 
-    head_cols = w_query.shape[1] // 4
     own_qkv = all_qkv.at[rank, shard]
     pairs = [(lambda r: small, all_small.at[rank, shard])]
     for i, weight in enumerate((w_query, w_key, w_value)):
-        own = own_qkv.at[:, pl.ds(i * head_cols, head_cols)]
-        pairs.append((columns(weight, head_cols), own))
+        pairs.append(
+            (columns(weight, head_cols), own_qkv.at[:, pl.ds(i * head_cols, head_cols)])
+        )
     deal_qkv = Deal(place, links, pairs)
-    gather = PlaneGather(place, links, tokens, all_tokens, 2)
-    deal_up = Deal(place, links, [(columns(w_up, w_up.shape[1] // 4), all_up.at[rank, shard])])
-
+    gather = PlaneGather(place, links, tokens, tokens_v, 2)
+    deal_up = Deal(place, links, [(columns(w_up, w_up.shape[1] // ranks), all_up.at[rank, shard])])
     links.keep(w_out, all_out.at[shard])
     links.keep(w_down, all_down.at[shard])
-    chain_out = Chain(place, links, w_out, lambda f: all_out.at[f])
-    deal_qkv.arrive()
+    out_slot = lambda f: all_out.at[f]
+    down_slot = lambda f: all_down.at[f]
     small_slot = lambda f: all_small.at[:, f]
     qkv_slot = lambda f: all_qkv.at[:, f]
     up_slot = lambda f: all_up.at[:, f]
+    chain_out = Chain(place, links, w_out, out_slot)
+    deal_qkv.arrive()
     chain_small = Chain(place, links, small_slot(shard), small_slot)
     chain_qkv = Chain(place, links, qkv_slot(shard), qkv_slot)
+    chain_small.step(1)
     gather.relay(0)
+    chain_small.step(2)
+    chain_out.step(1)
+    chain_small.step(3)
     gather.relay(1)
+    chain_qkv.step(1)
+    chain_small.finish()
+    chain_out.step(2)
+
+    def wide(rows):
+        spread = jnp.dot(rows, comb[...], preferred_element_type=jnp.float32)
+        return jnp.sum(spread * mask[...], axis=0, keepdims=True)
+
+    devices = ranks * 2 * chips
+    for i in range(5):
+        gains[i : i + 1] = wide(all_small[:, :, i].reshape(devices, 128))
+    up_rows = all_small[rank, :, 5:9].astype(jnp.float32).reshape(devices, 128)
+    gains[5:6] = wide(up_rows.astype(jnp.bfloat16))
+    gains[6:8] = jnp.zeros((2, model_width), jnp.float32)
+
+    def norm_block(r):
+        def rows_of(cut):
+            value, unused = normed(tokens_v[r, cut].astype(jnp.float32))
+            attn_v[r, cut] = (value * gains[0:1] + gains[1:2]).astype(jnp.bfloat16)
+
+        in_rows(tok_rows, 64, rows_of)
+
+    for copy in links.open_near:
+        copy.arrive()
+    norm_block(rank)
+    norm_block(place.first)
+    chain_qkv.step(2)
     deal_up.arrive()
     chain_up = Chain(place, links, up_slot(shard), up_slot)
-    chain_down = Chain(place, links, w_down, lambda f: all_down.at[f])
-
+    gather.finish()
+    norm_block(place.second)
+    norm_block(place.across)
+    links.keep(tokens_v, all_tokens)
+    links.keep(attn_v, attn_in)
+    chain_out.step(3)
+    chain_out.finish()
+    load_out = links.keep(all_out, out_v)
+    chain_qkv.step(3)
+    chain_qkv.finish()
+    load_qkv = links.keep(all_qkv, qkv_v)
     links.keep(suffix.at[block_of(rank)], incoming.at[0, rank])
     links.keep(suffix.at[1], incoming.at[1, rank], rank == 0)
     dealt = []
@@ -769,123 +860,484 @@
         dealt.append(
             Message(links, suffix.at[block_of(r)], incoming.at[0, rank], place.at(rank=r))
         )
-        dealt.append(
+    load_qkv.arrive()
+
+    def project(r, carry):
+        rows = pl.ds(pl.multiple_of(r * tok_rows, tok_rows), tok_rows)
+        for part in range(3):
+            cut = slice(part * head_cols, (part + 1) * head_cols)
+            weight = qkv_v[:, :, :, cut].reshape(model_width, head_cols)
+            value = jnp.dot(attn_v[r], weight, preferred_element_type=jnp.float32)
+            if part < 2:
+                turned = []
+                for h in range(heads):
+                    head = value[:, h * HEAD_DIM : (h + 1) * HEAD_DIM]
+                    turned.append(turn_half(head, cosine[rows], sine[rows]))
+                value = jnp.concatenate(turned, axis=1)
+                if part == 0:
+                    value = value * HEAD_DIM ** (-0.5)
+            rot_v[r, :, cut] = value.astype(jnp.bfloat16)
+        return carry
+
+    lax.fori_loop(0, ranks, project, 0)
+    links.keep(rot_v, qkv_rot)
+    chain_up.step(1)
+    load_out.arrive()
+
+    def attend_block(r):
+        def head(h, carry):
+            def part(i):
+                return pl.ds(pl.multiple_of(i * head_cols + h * HEAD_DIM, HEAD_DIM), HEAD_DIM)
+
+            scores = back_product(rot_v[r, :, part(0)], rot_v[:, :, part(1)].reshape(-1, HEAD_DIM))
+            row = lax.broadcasted_iota(jnp.int32, scores.shape, 0) + r * tok_rows
+            column = lax.broadcasted_iota(jnp.int32, scores.shape, 1)
+            scores = jnp.where(row >= column, scores, masked_score)
+            raised = jnp.exp(scores - jnp.max(scores, axis=-1, keepdims=True))
+            scale = 1.0 / jnp.sum(raised, axis=-1, keepdims=True)
+            probs = (raised * scale).astype(jnp.bfloat16)
+            mixed = product(probs, rot_v[:, :, part(2)].reshape(-1, HEAD_DIM))
+            mixed_v[r, :, part(0)] = mixed.astype(jnp.bfloat16)
+            return carry
+
+        lax.fori_loop(0, heads, head, 0)
+        weight = out_v[...].reshape(head_cols, model_width)
+        partial[r] = product(mixed_v[r], weight).astype(jnp.bfloat16)
+
+    scatter = PlaneScatter(place, links, partial, landing, passing)
+    attend_block(place.across)
+    scatter.send_far()
+    attend_block(place.first)
+    scatter.send_near()
+    chain_up.step(2)
+    chain_down = Chain(place, links, w_down, down_slot)
+    attend_block(place.second)
+    scatter.relay()
+    attend_block(rank)
+    links.keep(mixed_v, mixed_low)
+    chain_up.step(3)
+    chain_down.step(1)
+    scatter.settle()
+
+    def second_norm(cut):
+        value = scatter.total(cut) + tokens_v[rank, cut].astype(jnp.float32)
+        hidden[cut] = value
+        value, unused = normed(value)
+        ffn_v[cut] = (value * gains[2:3] + gains[3:4]).astype(jnp.bfloat16)
+
+    in_rows(tok_rows, 64, second_norm)
+    gather = PlaneGather(place, links, ffn_v, all_ffn_in, 2)
+    dealt_more = []
+    for r in (place.first, place.second, place.across):
+        dealt_more.append(
             Message(links, suffix.at[1], incoming.at[1, rank], place.at(rank=r), r == 0, rank == 0)
         )
-    for chain in (chain_out, chain_small, chain_qkv, chain_up, chain_down):
-        for s in range(1, chips):
-            chain.step(s)
-        chain.finish()
+    chain_down.step(2)
+    gather.relay(0)
+    gather.relay(1)
+    chain_up.finish()
+    chain_down.step(3)
     gather.finish()
-    for message in dealt:
+    chain_down.finish()
+    for message in dealt + dealt_more:
         message.arrive()
     links.drain()
 
 
-def block_of(r):
-    return jnp.where(r == 0, 0, jnp.minimum(r + 1, GRAN - 1))
-
-
-def scatter_kernel(chips, partial, total, landing, turn, send, recv, near):
+def middle_kernel(
+    chips,
+    all_ffn_in,
+    incoming,
+    w_up,
+    w_down,
+    hidden,
+    cotangent_sum,
+    gains,
+    grad_hidden,
+    sums,
+    share_down,
+    share_up,
+    terms,
+    ffn_v,
+    csum_v,
+    up_v,
+    down_v,
+    gated_v,
+    grad_v,
+    part_down,
+    other_down,
+    other_up,
+    terms_v,
+    partial,
+    landing,
+    passing,
+    send,
+    recv,
+    near,
+):
     place = Place(chips)
     links = Links(send, recv, near)
-    place.greet(plane=True)
-    scatter = PlaneScatter(place, links, partial, landing, turn)
+    rank = place.rank
+    ranks, tok_rows, model_width = ffn_v.shape
+    ff_cols = up_v.shape[-1]
+    half = ff_cols // 2
+    load_up = links.keep(w_up, up_v)
+    order = (place.across, place.first, place.second, rank)
+    load_ffn = [links.keep(all_ffn_in.at[t], ffn_v.at[t]) for t in order]
+    load_down = links.keep(w_down, down_v)
+    load_csum = [links.keep(incoming.at[0, t], csum_v.at[0, t]) for t in order]
+    load_more = links.keep(incoming.at[1], csum_v.at[1], rank == 0)
+    place.greet(plane=True, sibling=True)
+    slots = (0, jnp.where(rank == 0, 1, 0))
+    sums[...] = jnp.zeros_like(sums)
+    load_up.arrive()
+    scatter = PlaneScatter(place, links, partial, landing, passing)
+
+    def block(k):
+        t = order[k]
+        load_ffn[k].arrive()
+        for i in range(2):
+            cut = slice(i * half, (i + 1) * half)
+            weight = up_v[:, :, :, :, cut].reshape(model_width, half)
+            pre = product(ffn_v[t], weight) + gains[5:6, cut]
+            square = pre * pre
+            tangent = jnp.tanh(0.7978845608028654 * pre * (1.0 + 0.044715 * square))
+            gated_v[t, :, cut] = (0.5 * pre * (1.0 + tangent)).astype(jnp.bfloat16)
+            slope = 0.5 * (1.0 + tangent) + 0.5 * pre * (1.0 - tangent * tangent) * (
+                0.7978845608028654 * (1.0 + 3.0 * 0.044715 * square)
+            )
+            if k == 0 and i == 0:
+                load_down.arrive()
+                load_more.arrive()
+            if i == 0:
+                load_csum[k].arrive()
+            weight = down_v[4 * i : 4 * i + 4].reshape(half, model_width)
+            grad = back_product(csum_v[slots[i], t], weight) * slope
+            grad_v[t, :, cut] = grad.astype(jnp.bfloat16)
+            sums[3:4, cut] += jnp.sum(grad, axis=0, keepdims=True)
+
+        def back(i, carry):
+            own = model_width // ranks
+            value = back_product(grad_v[t], up_v[i].reshape(own, ff_cols))
+            partial[t, :, pl.ds(pl.multiple_of(i * own, 128), own)] = value.astype(jnp.bfloat16)
+            return carry
+
+        lax.fori_loop(0, ranks, back, 0)
+
+    block(0)
+    scatter.send_far()
+    block(1)
+    scatter.send_near()
+    block(2)
     scatter.relay()
-    total[...] = scatter.total()
+    block(3)
+
+    def down_tile(i, carry):
+        rows = ff_cols // ranks
+        left = gated_v[:, :, pl.ds(pl.multiple_of(i * rows, 128), rows)].reshape(-1, rows)
+        slot = jnp.where(i < 2, slots[0], slots[1])
+        value = gram_product(left, csum_v[slot].reshape(-1, model_width))
+        part_down[0, i] = value.astype(jnp.bfloat16).reshape(part_down.shape[2:])
+        return carry
+
+    lax.fori_loop(0, ranks, down_tile, 0)
+    beside_down = Beside(place, links, part_down, other_down)
+
+    def up_tile(i, carry):
+        rows = model_width // ranks
+        left = ffn_v[:, :, pl.ds(pl.multiple_of(i * rows, 128), rows)].reshape(-1, rows)
+        value = gram_product(left, grad_v[...].reshape(-1, ff_cols))
+        up_v[i] = value.astype(jnp.bfloat16).reshape(up_v.shape[1:])
+        return carry
+
+    lax.fori_loop(0, ranks, up_tile, 0)
+    beside_up = Beside(place, links, up_v, other_up)
+    beside_down.add()
+    links.keep(part_down.at[:, :, place.core], share_down)
+
+    def term_tile(t, carry):
+        low_term = product(gated_v[t, :, :half], down_v[:4].reshape(half, model_width))
+        high_term = product(gated_v[t, :, half:], down_v[4:].reshape(half, model_width))
+        terms_v[1, t] = high_term.astype(jnp.bfloat16)
+        low_term = low_term + high_term * jnp.where(rank == 0, 0.0, 1.0)
+        terms_v[0, t] = low_term.astype(jnp.bfloat16)
+        return carry
+
+    lax.fori_loop(0, ranks, term_tile, 0)
+    links.keep(terms_v, terms)
+    beside_up.add()
+    links.keep(up_v.at[:, :, place.core], share_up)
+    scatter.settle()
+
+    def norm_back(cut):
+        value, inverse = normed(hidden[cut])
+        grad = scatter.total(cut)
+        sums[0:1] += jnp.sum(grad * value, axis=0, keepdims=True)
+        sums[1:2] += jnp.sum(grad, axis=0, keepdims=True)
+        sums[2:3] += jnp.sum(cotangent_sum[cut], axis=0, keepdims=True)
+        grad_hidden[cut] = cotangent_sum[cut] + norm_backward(grad, value, inverse, gains[2:3])
+
+    in_rows(tok_rows, 64, norm_back)
     links.drain()
 
 
-def spread_kernel(chips, block, blocks, send, recv, near):
+def last_kernel(
+    chips,
+    branch,
+    share_down,
+    share_up,
+    terms,
+    qkv_rot,
+    mixed_low,
+    w_out,
+    w_qkv,
+    attn_in,
+    all_tokens,
+    grad_hidden,
+    hidden,
+    gains,
+    sums,
+    comb,
+    mask,
+    cosine,
+    sine,
+    activations,
+    grad_tokens,
+    sum_down,
+    sum_out,
+    sum_up,
+    sum_qkv,
+    sum_small,
+    branch_v,
+    rot_v,
+    mixed_v,
+    grad_mixed_v,
+    out_v,
+    qkv_v,
+    attn_v,
+    tokens_v,
+    grad_v,
+    key_sum,
+    value_sum,
+    partial,
+    landing,
+    passing,
+    term_in,
+    extra_in,
+    mine_down,
+    land_down,
+    mine_up,
+    land_up,
+    turn_up,
+    part_out,
+    other_out,
+    land_out,
+    part_qkv,
+    other_qkv,
+    land_qkv,
+    turn_qkv,
+    part_small,
+    other_small,
+    land_small,
+    turn_small,
+    land_sums,
+    more_sums,
+    send,
+    recv,
+    near,
+):
     place = Place(chips)
     links = Links(send, recv, near)
-    place.greet(plane=True)
-    gather = PlaneGather(place, links, block, blocks, 2)
+    rank, z = place.rank, place.z
+    ranks, tok_rows, model_width = branch_v.shape
+    head_cols = mixed_v.shape[2]
+    heads = head_cols // HEAD_DIM
+    load_out = links.keep(w_out, out_v)
+    load_mixed = links.keep(mixed_low, mixed_v)
+    load_rot = links.keep(qkv_rot, rot_v)
+    load_qkv = links.keep(w_qkv, qkv_v)
+    load_attn = links.keep(attn_in, attn_v)
+    load_tokens = links.keep(all_tokens, tokens_v)
+    load_down = links.keep(share_down.at[:, z], mine_down)
+    load_up = links.keep(share_up.at[:, z], mine_up)
+    place.greet(plane=True, sibling=True, ring=True)
+    gather = PlaneGather(place, links, branch, branch_v, 2)
+    along_down = Along(place, links, lambda there: share_down.at[:, there], land_down)
+    along_up = Along(place, links, lambda there: share_up.at[:, there], land_up)
+    load_out.arrive()
+
+    def mix_back(t):
+        weight = out_v[...].reshape(head_cols, model_width)
+        grad_mixed_v[t] = back_product(branch_v[t], weight).astype(jnp.bfloat16)
+
+    links.open_near[8].arrive()
+    mix_back(rank)
     gather.relay(0)
     gather.relay(1)
+    mix_back(place.first)
     gather.finish()
-    links.drain()
-
-
-def middle_kernel(
-    chips,
-    branch,
-    terms,
-    part_down,
-    part_up,
-    all_branch,
-    term_in,
-    extra_in,
-    sum_down,
-    sum_up,
-    *scratch,
-):
-    own_down, other_down, land_down, own_up, other_up, land_up, turn, send, recv, near = scratch
-    place = Place(chips)
-    links = Links(send, recv, near)
-    place.greet(plane=True, sibling=True, ring=True)
-    rank = place.rank
-    collect_down = Collect(place, links, part_down, own_down, other_down, land_down)
-    collect_up = Collect(place, links, part_up, own_up, other_up, land_up)
-    gather = PlaneGather(place, links, branch, all_branch, 2)
-    collect_down.send()
-    collect_up.send()
-    gather.relay(0)
-    gather.relay(1)
+    mix_back(place.second)
+    mix_back(place.across)
     links.keep(terms.at[0, rank], term_in.at[rank])
     links.keep(terms.at[1, rank], extra_in, rank == 0)
     dealt = []
     for r in (place.first, place.second, place.across):
         dealt.append(Message(links, terms.at[0, r], term_in.at[rank], place.at(rank=r)))
-        dealt.append(
+    load_mixed.arrive()
+    value = gram_product(
+        mixed_v[...].reshape(-1, head_cols), branch_v[...].reshape(-1, model_width)
+    )
+    part_out[0] = value.astype(jnp.bfloat16).reshape(part_out.shape[1:])
+    beside_out = Beside(place, links, part_out, other_out)
+    load_rot.arrive()
+
+    def head(h, carry):
+        def part(i):
+            return pl.ds(pl.multiple_of(i * head_cols + h * HEAD_DIM, HEAD_DIM), HEAD_DIM)
+
+        for t in range(ranks - 1, -1, -1):
+            count = t + 1
+            keys = rot_v[:count, :, part(1)].reshape(-1, HEAD_DIM)
+            values = rot_v[:count, :, part(2)].reshape(-1, HEAD_DIM)
+            queries = rot_v[t, :, part(0)]
+            grad_mixed = grad_mixed_v[t, :, part(0)]
+            scores = back_product(queries, keys)
+            row = lax.broadcasted_iota(jnp.int32, scores.shape, 0) + t * tok_rows
+            column = lax.broadcasted_iota(jnp.int32, scores.shape, 1)
+            scores = jnp.where(row >= column, scores, masked_score)
+            raised = jnp.exp(scores - jnp.max(scores, axis=-1, keepdims=True))
+            probs = raised * (1.0 / jnp.sum(raised, axis=-1, keepdims=True))
+            delta = jnp.sum(
+                grad_mixed.astype(jnp.float32) * mixed_v[t, :, part(0)].astype(jnp.float32),
+                axis=-1,
+                keepdims=True,
+            )
+            grad_scores = (probs * (back_product(grad_mixed, values) - delta)).astype(jnp.bfloat16)
+            rows = pl.ds(t * tok_rows, tok_rows)
+            grad_query = product(grad_scores, keys)
+            grad_query = turn_half(grad_query, cosine[rows], -sine[rows]) * HEAD_DIM ** (-0.5)
+            grad_v[t, :, part(0)] = grad_query.astype(jnp.bfloat16)
+            grad_key = gram_product(grad_scores, queries)
+            grad_value = gram_product(probs.astype(jnp.bfloat16), grad_mixed)
+            seen = count * tok_rows
+            if t == ranks - 1:
+                key_sum[...] = grad_key
+                value_sum[...] = grad_value
+            else:
+                key_sum[:seen] += grad_key
+                value_sum[:seen] += grad_value
+        grad_key = turn_half(key_sum[...], cosine[...], -sine[...]).astype(jnp.bfloat16)
+        grad_v[:, :, part(1)] = grad_key.reshape(ranks, tok_rows, HEAD_DIM)
+        grad_value = value_sum[...].astype(jnp.bfloat16)
+        grad_v[:, :, part(2)] = grad_value.reshape(ranks, tok_rows, HEAD_DIM)
+        return carry
+
+    lax.fori_loop(0, heads, head, 0)
+    beside_out.add()
+    along_out = Along(place, links, lambda there: part_out.at[:, there, place.core], land_out)
+    load_qkv.arrive()
+    load_attn.arrive()
+    load_tokens.arrive()
+
+    def qkv_tile(i, carry):
+        rows = model_width // ranks
+        left = attn_v[:, :, pl.ds(pl.multiple_of(i * rows, 128), rows)].reshape(-1, rows)
+        value = gram_product(left, grad_v[...].reshape(-1, 3 * head_cols))
+        part_qkv[i] = value.astype(jnp.bfloat16).reshape(part_qkv.shape[1:])
+        return carry
+
+    lax.fori_loop(0, ranks, qkv_tile, 0)
+    beside_qkv = Beside(place, links, part_qkv, other_qkv)
+    scatter = PlaneScatter(place, links, partial, landing, passing)
+    more_sums[...] = jnp.zeros_like(more_sums)
+
+    def attn_back(t):
+        def tile(i, carry):
+            own = model_width // ranks
+            value = back_product(grad_v[t], qkv_v[i].reshape(own, 3 * head_cols))
+            partial[t, :, pl.ds(pl.multiple_of(i * own, 128), own)] = value.astype(jnp.bfloat16)
+            return carry
+
+        lax.fori_loop(0, ranks, tile, 0)
+
+        def count(cut):
+            value, unused = normed(tokens_v[t, cut].astype(jnp.float32))
+            grad = partial[t, cut].astype(jnp.float32)
+            more_sums[0:1] += jnp.sum(grad * value, axis=0, keepdims=True)
+            more_sums[1:2] += jnp.sum(grad, axis=0, keepdims=True)
+
+        return count
+
+    count_across = attn_back(place.across)
+    scatter.send_far()
+    count_first = attn_back(place.first)
+    scatter.send_near()
+    beside_qkv.add()
+    along_qkv = Along(place, links, lambda there: part_qkv.at[:, there, place.core], land_qkv)
+    count_second = attn_back(place.second)
+    scatter.relay()
+    count_own = attn_back(rank)
+    for count in (count_across, count_first, count_second, count_own):
+        in_rows(tok_rows, 64, count)
+
+    def pieces(row):
+        spread = (row * mask[...]).astype(jnp.float32)
+        return lax.dot_general(
+            spread,
+            comb[...].astype(jnp.float32),
+            (((1,), (1,)), ((), ())),
+            precision=lax.Precision.HIGHEST,
+            preferred_element_type=jnp.float32,
+        )
+
+    part_small[...] = jnp.zeros_like(part_small)
+    rows = (more_sums[0:1], more_sums[1:2], sums[0:1], sums[1:2], sums[2:3])
+    for k, row in enumerate(rows):
+        part_small[:, :, :, k] = pieces(row).reshape(ranks, chips, 2, 128)
+    part_small[rank, :, :, 5:9] = pieces(sums[3:4]).reshape(chips, 2, 4, 128)
+    beside_small = Beside(place, links, part_small, other_small)
+    dealt_more = []
+    for r in (place.first, place.second, place.across):
+        dealt_more.append(
             Message(links, terms.at[1, r], extra_in, place.at(rank=r), rank == 0, r == 0)
         )
-    sum_down[...] = collect_down.total()[0]
-    turn[...] = collect_up.total().astype(jnp.bfloat16)
-    deal_up = Deal(
-        place, links, [(lambda r: turn.at[r], sum_up.at[rank])]
-    )
-    gather.finish()
-    for message in dealt:
+    load_down.arrive()
+    sum_down[...] = along_down.total(mine_down[...])[0]
+    load_up.arrive()
+    turn_up[...] = along_up.total(mine_up[...]).astype(jnp.bfloat16)
+    deal_up = Deal(place, links, [(lambda r: turn_up.at[r], sum_up.at[rank])])
+    beside_small.add()
+    along_small = Along(place, links, lambda there: part_small.at[:, there, place.core], land_small)
+    sum_out[...] = along_out.total(part_out[:, z, place.core])[0]
+    scatter.settle()
+
+    def norm_back(cut):
+        value, inverse = normed(tokens_v[rank, cut].astype(jnp.float32))
+        grad = norm_backward(scatter.total(cut), value, inverse, gains[0:1])
+        grad_tokens[cut] = (grad_hidden[cut] + grad).astype(jnp.bfloat16)
+
+    in_rows(tok_rows, 64, norm_back)
+    turn_small[...] = along_small.total(part_small[:, z, place.core])
+    deal_small = Deal(place, links, [(lambda r: turn_small.at[r], land_sums.at[rank])])
+    turn_qkv[...] = along_qkv.total(part_qkv[:, z, place.core]).astype(jnp.bfloat16)
+    deal_qkv = Deal(place, links, [(lambda r: turn_qkv.at[r], sum_qkv.at[rank])])
+    for copy in links.open_near:
+        copy.arrive()
+    for message in dealt + dealt_more:
         message.arrive()
+
+    def add_terms(cut):
+        total = hidden[cut] + gains[4:5] + term_in[0, cut].astype(jnp.float32)
+        activations[0, cut] = total.astype(jnp.bfloat16)
+        total = total + extra_in[cut].astype(jnp.float32)
+        activations[1, cut] = total.astype(jnp.bfloat16)
+        total = total + term_in[1, cut].astype(jnp.float32)
+        activations[2, cut] = total.astype(jnp.bfloat16)
+        total = total + term_in[2, cut].astype(jnp.float32) + term_in[3, cut].astype(jnp.float32)
+        activations[3, cut] = total.astype(jnp.bfloat16)
+
+    in_rows(tok_rows, 64, add_terms)
     deal_up.arrive()
-    links.drain()
-
-
-def last_kernel(
-    chips,
-    partial,
-    part_out,
-    part_qkv,
-    part_small,
-    total,
-    sum_out,
-    sum_qkv,
-    sum_small,
-    *scratch,
-):
-    landing, passing = scratch[:2]
-    own_out, other_out, land_out, own_qkv, other_qkv, land_qkv = scratch[2:8]
-    own_small, other_small, land_small, turn, turn_small, land_sums = scratch[8:14]
-    send, recv, near = scratch[14:]
-    place = Place(chips)
-    links = Links(send, recv, near)
-    place.greet(plane=True, sibling=True, ring=True)
-    rank = place.rank
-    collect_small = Collect(place, links, part_small, own_small, other_small, land_small)
-    collect_qkv = Collect(place, links, part_qkv, own_qkv, other_qkv, land_qkv)
-    collect_out = Collect(place, links, part_out, own_out, other_out, land_out)
-    scatter = PlaneScatter(place, links, partial, landing, passing)
-    collect_small.send()
-    collect_qkv.send()
-    collect_out.send()
-    scatter.relay()
-    turn_small[...] = collect_small.total()
-    deal_small = Deal(place, links, [(lambda r: turn_small.at[r], land_sums.at[rank])])
-    turn[...] = collect_qkv.total().astype(jnp.bfloat16)
-    deal_qkv = Deal(place, links, [(lambda r: turn.at[r], sum_qkv.at[rank])])
-    sum_out[...] = collect_out.total()[0]
-    total[...] = scatter.total()
     deal_small.arrive()
     sum_small[...] = land_sums[0] + land_sums[1] + land_sums[2] + land_sums[3]
     deal_qkv.arrive()
@@ -904,7 +1356,7 @@
         out_specs=out_specs,
         scratch_shapes=scratch + LINK_SCRATCH,
         compiler_params=pltpu.CompilerParams(
-            collective_id=number, has_side_effects=True, vmem_limit_bytes=60 * 2**20
+            collective_id=number, has_side_effects=True, vmem_limit_bytes=63 * 2**20
         ),
     )(*operands)
 
@@ -945,256 +1397,229 @@
     suffix = [grads_out[GRAN - 1]]
     for level_idx in range(GRAN - 2, -1, -1):
         suffix.insert(0, suffix[0] + grads_out[level_idx])
-    grad_hidden = suffix[0]
+    cotangent_sum = suffix[0]
     suffix = jnp.stack([s.astype(jnp.bfloat16) for s in suffix])
 
-    small = jnp.concatenate([norm1_gain, norm1_bias, norm2_gain, norm2_bias, down_bias, up_bias])
-    small = jnp.pad(small, (0, 16 * 128 - small.shape[0])).reshape(16, 128)
+    rows = [
+        jnp.pad(v.reshape(-1, own), ((0, 0), (0, 128 - own)))
+        for v in (norm1_gain, norm1_bias, norm2_gain, norm2_bias, down_bias, up_bias)
+    ]
+    small = jnp.pad(jnp.concatenate(rows), ((0, 16 - 5 - up_bias.shape[0] // own), (0, 0)))
+    column = jnp.arange(model_width, dtype=jnp.int32)
+    comb = (column[None, :] % own == jnp.arange(128, dtype=jnp.int32)[:, None]).astype(jnp.bfloat16)
+    mask = column[None, :] // own == jnp.arange(ranks * shards, dtype=jnp.int32)[:, None]
+    mask = mask.astype(jnp.float32)
+    cosine, sine = rotary_tables(jnp.arange(seq_len).astype(jnp.float32), HEAD_DIM // 2)
+    cosine, sine = cosine[:, 0], sine[:, 0]
+    cosine = jnp.concatenate([cosine, cosine], axis=1)
+    sine = jnp.concatenate([-sine, sine], axis=1)
     own_tokens = tokens.reshape(tok_rows, model_width)
-    all_tokens, incoming, all_small, w_qkv, w_out, w_up, w_down = connected(
-        functools.partial(gather_kernel, chips),
+    blocks_low = array((ranks, tok_rows, model_width))
+    down_rows = down_weight.shape[0]
+    vmem = pltpu.VMEM
+    (
+        all_tokens,
+        attn_in,
+        qkv_rot,
+        mixed_low,
+        hidden,
+        ffn_in,
+        gains,
+        incoming,
+        w_qkv,
+        w_out,
+        w_up,
+        w_down,
+    ) = connected(
+        functools.partial(forward_kernel, chips),
         1,
         (
-            array((ranks, tok_rows, model_width)),
+            blocks_low,
+            blocks_low,
+            array((ranks, tok_rows, 3 * head_cols)),
+            array((ranks, tok_rows, head_cols)),
+            array((tok_rows, model_width), jnp.float32),
+            blocks_low,
+            array((8, model_width), jnp.float32),
             array((2, ranks, tok_rows, model_width)),
-            array((ranks, shards, 16, 128)),
             array((ranks, shards, own, 3 * head_cols)),
             array((shards, own, model_width)),
             array((ranks, shards, own, ff_cols)),
-            array((shards, down_weight.shape[0], model_width)),
+            array((shards, down_rows, model_width)),
         ),
-        [ANY] * 7,
-        [ANY] * 9,
-        [],
-        (own_tokens, suffix, small, query_weight, key_weight, value_weight, out_weight, up_weight, down_weight),
-    )
-    small = all_small.reshape(ranks * shards, 16 * 128)[:, : 5 * own + ff_cols // shards].astype(jnp.float32)
-    gain_one, bias_one, gain_two, bias_two, b_down = (
-        small[:, i * own : (i + 1) * own].reshape(model_width) for i in range(5)
-    )
-    b_up_all = small[:, 5 * own :].reshape(ranks, ff_cols)
-    b_up = lax.dynamic_index_in_dim(b_up_all, rank, 0, keepdims=False)
-    w_qkv = w_qkv.reshape(model_width, 3 * head_cols)
-    w_up = w_up.reshape(model_width, ff_cols)
-    w_out = w_out.reshape(head_cols, model_width)
-    w_down = w_down.reshape(ff_cols, model_width)
-    all_tokens = all_tokens.reshape(seq_len, model_width).astype(jnp.float32)
-    normed_all, unused = norm_parts(all_tokens)
-    attn_in = (normed_all * gain_one + bias_one).astype(jnp.bfloat16)
-    qkv = product(attn_in, w_qkv)
-    queries = qkv[:, :head_cols].reshape(seq_len, heads, HEAD_DIM)
-    key_raw = qkv[:, head_cols : 2 * head_cols].reshape(seq_len, heads, HEAD_DIM)
-    values = qkv[:, 2 * head_cols :].astype(jnp.bfloat16).reshape(seq_len, heads, HEAD_DIM)
-    positions = jnp.arange(seq_len, dtype=jnp.int32)
-    cosine, sine = rotary_tables(positions.astype(jnp.float32), HEAD_DIM // 2)
-    q_rot = (rotate(queries, cosine, sine) * scaling).astype(jnp.bfloat16)
-    k_rot = rotate(key_raw, cosine, sine).astype(jnp.bfloat16)
-    visible = (positions[:, None] >= positions[None, :])[None]
-
-    def weigh(log_total=None):
-        scores = jnp.einsum("qhd,khd->hqk", q_rot, k_rot, preferred_element_type=jnp.float32)
-        scores = jnp.where(visible, scores, masked_score)
-        if log_total is None:
-            top = jnp.max(scores, axis=-1)
-            log_total = top + jnp.log(jnp.sum(jnp.exp(scores - top[..., None]), axis=-1))
-        return jnp.exp(scores - log_total[..., None]), log_total
-
-    probs, log_total = weigh()
-    mixed = jnp.einsum(
-        "hqk,khd->qhd", probs.astype(jnp.bfloat16), values, preferred_element_type=jnp.float32
-    )
-    mixed_low = mixed.reshape(seq_len, head_cols).astype(jnp.bfloat16)
-
-    blocks_low = array((ranks, tok_rows, model_width))
-
-    def add_up(number, partial):
-        return connected(
-            functools.partial(scatter_kernel, chips),
-            number,
-            array((tok_rows, model_width), jnp.float32),
-            ON_CORE,
-            [ON_CORE],
-            [
-                pltpu.VMEM((3, tok_rows, model_width), jnp.bfloat16),
-                pltpu.VMEM((tok_rows, model_width), jnp.bfloat16),
-            ],
-            (partial.astype(jnp.bfloat16).reshape(ranks, tok_rows, model_width),),
-        )
-
-    inputs = own_tokens.astype(jnp.float32)
-    hidden = inputs + add_up(2, product(mixed_low, w_out))
-    normed_two, inverse_two = norm_parts(hidden)
-    ffn_in_own = (normed_two * gain_two + bias_two).astype(jnp.bfloat16)
-    ffn_in = connected(
-        functools.partial(spread_kernel, chips), 3, blocks_low, ANY, [ANY], [], (ffn_in_own,)
-    ).reshape(seq_len, model_width)
-    preact = product(ffn_in, w_up) + b_up
-    gated = gelu_value(preact).astype(jnp.bfloat16)
-
-    half = ff_cols // 2
-    low_term = product(gated[:, :half], w_down[:half])
-    high_term = product(gated[:, half:], w_down[half:])
-    terms = jnp.stack(
+        [ANY] * 4 + [ON_CORE, ANY, ON_CORE] + [ANY] * 5,
+        [ANY] * 9 + [ON_CORE] * 4,
         [
-            (low_term + jnp.where(rank == 0, 0.0, high_term)).astype(jnp.bfloat16),
-            high_term.astype(jnp.bfloat16),
-        ]
-    ).reshape(2, ranks, tok_rows, model_width)
-    split_grads = [
-        incoming[0].reshape(seq_len, model_width),
-        jnp.where(rank == 0, incoming[1], incoming[0]).reshape(seq_len, model_width),
-    ]
-    grad_gated = jnp.concatenate(
-        [back_product(split_grads[i], w_down[i * half : (i + 1) * half]) for i in range(2)],
-        axis=1,
-    )
-    grad_pre_wide = grad_gated * gelu_grad(preact)
-    grad_pre = grad_pre_wide.astype(jnp.bfloat16)
-    grad_up_bias = jnp.sum(grad_pre_wide, axis=0)
-    grad_ffn_in = add_up(4, back_product(grad_pre, w_up))
-
-    part_down = jnp.concatenate(
-        [gram_product(gated[:, i * half : (i + 1) * half], split_grads[i]) for i in range(2)],
-        axis=0,
-    ).astype(jnp.bfloat16)
-    part_up = gram_product(ffn_in, grad_pre).astype(jnp.bfloat16)
-    grad_down_bias = jnp.sum(grad_hidden, axis=0)
-    grad_gain_two = jnp.sum(grad_ffn_in * normed_two, axis=0)
-    grad_bias_two = jnp.sum(grad_ffn_in, axis=0)
-    grad_hidden = grad_hidden + norm_backward(grad_ffn_in, normed_two, inverse_two, gain_two)
-    down_rows = ff_cols // shards
-    grad_branch, term_in, extra_in, sum_down, sum_up = connected(
-        functools.partial(middle_kernel, chips),
-        5,
-        (
-            blocks_low,
-            blocks_low,
-            array((tok_rows, model_width)),
-            array((down_rows, model_width), jnp.float32),
-            array((ranks, own, ff_cols)),
-        ),
-        [ANY, ANY, ANY, ON_CORE, ANY],
-        [ANY] * 4,
-        collect_scratch(1, chips, down_rows, model_width, jnp.bfloat16)
-        + collect_scratch(ranks, chips, own, ff_cols, jnp.bfloat16)
-        + [pltpu.VMEM((ranks, own, ff_cols), jnp.bfloat16)],
-        (
-            grad_hidden.astype(jnp.bfloat16),
-            terms,
-            part_down.reshape(1, chips, 2, down_rows, model_width),
-            part_up.reshape(ranks, chips, 2, own, ff_cols),
-        ),
-    )
-    grad_branch = grad_branch.reshape(seq_len, model_width)
-    sum_up = sum_up.astype(jnp.float32).transpose(1, 0, 2).reshape(own, FF)
-    total = hidden + b_down + term_in[0].astype(jnp.float32)
-    result_list = [total.astype(jnp.bfloat16)]
-    total = total + extra_in.astype(jnp.float32)
-    result_list.append(total.astype(jnp.bfloat16))
-    total = total + term_in[1].astype(jnp.float32)
-    result_list.append(total.astype(jnp.bfloat16))
-    total = total + term_in[2].astype(jnp.float32) + term_in[3].astype(jnp.float32)
-    result_list.append(total.astype(jnp.bfloat16))
-    activations = jnp.stack(result_list).reshape(GRAN, 1, tok_rows, model_width)
-    part_out = gram_product(mixed_low, grad_branch).astype(jnp.bfloat16)
-    grad_mixed = (
-        back_product(grad_branch, w_out).astype(jnp.bfloat16).reshape(seq_len, heads, HEAD_DIM)
-    )
-    row_delta = jnp.einsum("qhd,qhd->hq", grad_mixed.astype(jnp.float32), mixed)
-    probs, unused = weigh(log_total)
-    grad_probs = jnp.einsum("qhd,khd->hqk", grad_mixed, values, preferred_element_type=jnp.float32)
-    grad_scores = (probs * (grad_probs - row_delta[..., None])).astype(jnp.bfloat16)
-    grad_q_rot = jnp.einsum(
-        "hqk,khd->qhd", grad_scores, k_rot, preferred_element_type=jnp.float32
-    )
-    grad_k_rot = jnp.einsum(
-        "hqk,qhd->khd", grad_scores, q_rot, preferred_element_type=jnp.float32
-    )
-    grad_values = jnp.einsum(
-        "hqk,qhd->khd", probs.astype(jnp.bfloat16), grad_mixed, preferred_element_type=jnp.float32
-    )
-    grad_qkv = jnp.concatenate(
-        [
-            rotate(grad_q_rot * scaling, cosine, -sine).reshape(seq_len, head_cols),
-            rotate(grad_k_rot, cosine, -sine).reshape(seq_len, head_cols),
-            grad_values.reshape(seq_len, head_cols),
-        ],
-        axis=1,
-    ).astype(jnp.bfloat16)
-    part_qkv = gram_product(attn_in, grad_qkv).astype(jnp.bfloat16)
-    partial = back_product(grad_qkv, w_qkv).astype(jnp.bfloat16)
-    sums = jnp.stack([grad_gain_two, grad_bias_two, grad_down_bias])
-    sums = sums.reshape(3, ranks, shards, own).transpose(1, 2, 0, 3).reshape(ranks, shards, 3 * own)
-    here = (jnp.arange(ranks) == rank).astype(jnp.float32)[:, None, None]
-    sums = jnp.concatenate([sums, here * grad_up_bias.reshape(1, shards, -1)], axis=2)
-    used = sums.shape[2]
-    sums = jnp.pad(sums, ((0, 0), (0, 0), (0, 1024 - used)))
-    grad_attn_in, sum_out, sum_qkv, sums = connected(
-        functools.partial(last_kernel, chips),
-        6,
-        (
-            array((tok_rows, model_width), jnp.float32),
-            array((own, model_width), jnp.float32),
-            array((ranks, own, 3 * head_cols)),
-            array((8, 128), jnp.float32),
-        ),
-        [ON_CORE, ON_CORE, ANY, ON_CORE],
-        [ON_CORE, ANY, ANY, ANY],
-        [
-            pltpu.VMEM((3, tok_rows, model_width), jnp.bfloat16),
-            pltpu.VMEM((tok_rows, model_width), jnp.bfloat16),
-        ]
-        + collect_scratch(1, chips, own, model_width, jnp.bfloat16)
-        + collect_scratch(ranks, chips, own, 3 * head_cols, jnp.bfloat16)
-        + collect_scratch(ranks, chips, 8, 128, jnp.float32)
-        + [
-            pltpu.VMEM((ranks, own, 3 * head_cols), jnp.bfloat16),
-            pltpu.VMEM((ranks, 8, 128), jnp.float32),
-            pltpu.VMEM((ranks, 8, 128), jnp.float32),
+            vmem((ranks, tok_rows, model_width), jnp.bfloat16),
+            vmem((ranks, tok_rows, model_width), jnp.bfloat16),
+            vmem((ranks, tok_rows, 3 * head_cols), jnp.bfloat16),
+            vmem((ranks, tok_rows, head_cols), jnp.bfloat16),
+            vmem((ranks, shards, own, 3 * head_cols), jnp.bfloat16),
+            vmem((shards, own, model_width), jnp.bfloat16),
+            vmem((ranks, tok_rows, model_width), jnp.bfloat16),
+            vmem((3, tok_rows, model_width), jnp.bfloat16),
+            vmem((tok_rows, model_width), jnp.bfloat16),
+            vmem((tok_rows, model_width), jnp.bfloat16),
+            vmem((ranks, shards, 16, 128), jnp.bfloat16),
         ],
         (
-            partial.reshape(ranks, tok_rows, model_width),
-            part_out.reshape(1, chips, 2, own, model_width),
-            part_qkv.reshape(ranks, chips, 2, own, 3 * head_cols),
-            sums.reshape(ranks, chips, 2, 8, 128),
+            own_tokens,
+            suffix,
+            small,
+            query_weight,
+            key_weight,
+            value_weight,
+            out_weight,
+            up_weight,
+            down_weight,
+            comb,
+            mask,
+            cosine,
+            sine,
         ),
     )
-    sums = sums.reshape(1024)
-    sum_gain_two, sum_bias_two, sum_down_bias = (sums[i * own : (i + 1) * own] for i in range(3))
-    sum_up_bias = sums[3 * own : used]
-    sum_qkv = sum_qkv.astype(jnp.float32).transpose(1, 0, 2)
+    low = jnp.bfloat16
+    f32 = jnp.float32
+    grad_hidden, sums, share_down, share_up, terms = connected(
+        functools.partial(middle_kernel, chips),
+        2,
+        (
+            array((tok_rows, model_width), f32),
+            array((8, model_width), f32),
+            array((1, chips, down_rows, model_width)),
+            array((ranks, chips, own, ff_cols)),
+            array((2, ranks, tok_rows, model_width)),
+        ),
+        [ON_CORE] * 2 + [ANY] * 3,
+        [ANY] * 4 + [ON_CORE] * 3,
+        [
+            vmem((ranks, tok_rows, model_width), low),
+            vmem((2, ranks, tok_rows, model_width), low),
+            vmem((ranks, chips, 2, own, ff_cols), low),
+            vmem((shards, down_rows, model_width), low),
+            vmem((ranks, tok_rows, ff_cols), low),
+            vmem((ranks, tok_rows, ff_cols), low),
+            vmem((1, chips, 2, down_rows, model_width), low),
+            vmem((1, chips, down_rows, model_width), low),
+            vmem((ranks, chips, own, ff_cols), low),
+            vmem((2, ranks, tok_rows, model_width), low),
+            vmem((ranks, tok_rows, model_width), low),
+            vmem((3, tok_rows, model_width), low),
+            vmem((tok_rows, model_width), low),
+        ],
+        (
+            ffn_in,
+            incoming,
+            w_up.reshape(ranks, chips, 2, own, ff_cols),
+            w_down,
+            hidden,
+            cotangent_sum,
+            gains,
+        ),
+    )
+    (
+        activations,
+        grad_inputs,
+        sum_down,
+        sum_out,
+        sum_up,
+        sum_qkv,
+        small_sums,
+    ) = connected(
+        functools.partial(last_kernel, chips),
+        3,
+        (
+            array((GRAN, tok_rows, model_width)),
+            array((tok_rows, model_width)),
+            array((down_rows, model_width), f32),
+            array((own, model_width), f32),
+            array((ranks, own, ff_cols)),
+            array((ranks, own, 3 * head_cols)),
+            array((16, 128), f32),
+        ),
+        [ON_CORE] * 4 + [ANY, ANY, ON_CORE],
+        [ANY] * 10 + [ON_CORE] * 8,
+        [
+            vmem((ranks, tok_rows, model_width), low),
+            vmem((ranks, tok_rows, 3 * head_cols), low),
+            vmem((ranks, tok_rows, head_cols), low),
+            vmem((ranks, tok_rows, head_cols), low),
+            vmem((shards, own, model_width), low),
+            vmem((ranks, shards, own, 3 * head_cols), low),
+            vmem((ranks, tok_rows, model_width), low),
+            vmem((ranks, tok_rows, model_width), low),
+            vmem((ranks, tok_rows, 3 * head_cols), low),
+            vmem((seq_len, HEAD_DIM), f32),
+            vmem((seq_len, HEAD_DIM), f32),
+            vmem((ranks, tok_rows, model_width), low),
+            vmem((3, tok_rows, model_width), low),
+            vmem((tok_rows, model_width), low),
+            vmem((ranks, tok_rows, model_width), low),
+            vmem((tok_rows, model_width), low),
+            vmem((1, down_rows, model_width), low),
+            vmem((chips - 1, 1, down_rows, model_width), low),
+            vmem((ranks, own, ff_cols), low),
+            vmem((chips - 1, ranks, own, ff_cols), low),
+            vmem((ranks, own, ff_cols), low),
+            vmem((1, chips, 2, own, model_width), low),
+            vmem((1, chips, own, model_width), low),
+            vmem((chips - 1, 1, own, model_width), low),
+            vmem((ranks, chips, 2, own, 3 * head_cols), low),
+            vmem((ranks, chips, own, 3 * head_cols), low),
+            vmem((chips - 1, ranks, own, 3 * head_cols), low),
+            vmem((ranks, own, 3 * head_cols), low),
+            vmem((ranks, chips, 2, 16, 128), f32),
+            vmem((ranks, chips, 16, 128), f32),
+            vmem((chips - 1, ranks, 16, 128), f32),
+            vmem((ranks, 16, 128), f32),
+            vmem((ranks, 16, 128), f32),
+            vmem((8, model_width), f32),
+        ],
+        (
+            grad_hidden.astype(low),
+            share_down,
+            share_up,
+            terms,
+            qkv_rot,
+            mixed_low,
+            w_out,
+            w_qkv,
+            attn_in,
+            all_tokens,
+            grad_hidden,
+            hidden,
+            gains,
+            sums,
+            comb,
+            mask,
+            cosine,
+            sine,
+        ),
+    )
+    activations = activations.reshape(GRAN, 1, tok_rows, model_width)
+    sum_up = sum_up.astype(f32).transpose(1, 0, 2).reshape(own, FF)
+    sum_qkv = sum_qkv.astype(f32).transpose(1, 0, 2)
     sum_query, sum_key, sum_value = (
         sum_qkv[:, :, i * head_cols : (i + 1) * head_cols].reshape(own, model_width)
         for i in range(3)
     )
-    normed_one, inverse_one = norm_parts(inputs)
-    grad_gain_one = jnp.sum(grad_attn_in * normed_one, axis=0)
-    grad_bias_one = jnp.sum(grad_attn_in, axis=0)
-    grad_inputs = grad_hidden + norm_backward(grad_attn_in, normed_one, inverse_one, gain_one)
-
-    sums_one = lax.psum_scatter(
-        jnp.concatenate(
-            [g.reshape(ranks * shards, own) for g in (grad_gain_one, grad_bias_one)], axis=1
-        ),
-        ("dp", "fsdp"),
-        scatter_dimension=0,
-        tiled=True,
-    ).reshape(2, own)
+    gain_sums = [small_sums[i, :own] for i in range(5)]
+    sum_up_bias = small_sums[5:9, :own].reshape(-1)
     return (
         activations,
-        grad_inputs.astype(jnp.bfloat16).reshape(1, tok_rows, model_width),
-        sums_one[0],
-        sums_one[1],
+        grad_inputs.reshape(1, tok_rows, model_width),
+        gain_sums[0],
+        gain_sums[1],
         sum_query,
         sum_key,
         sum_value,
         sum_out,
-        sum_gain_two,
-        sum_bias_two,
+        gain_sums[2],
+        gain_sums[3],
         sum_up,
         sum_up_bias,
         sum_down,
-        sum_down_bias,
+        gain_sums[4],
     )
 
 

time: 696 us -> 442 us (0.64)
  matrix products: 113 us -> 0 us
  blocking collectives: 42.1 us -> 0 us
  other arithmetic: 53.9 us -> 13.4 us
  local copies, waits for them, and re-layouts: 47.7 us -> 15.5 us
  Pallas kernels: 432 us -> 408 us
    dot_general x21 -> x0, matrix products: 113 us -> none  [the longest x5 29.6 us: product(): return jnp.dot(left, right, preferred_element_type=jnp.float32)]
    unnamed x1 -> x0, blocking collectives: 42.1 us -> none
    pallas_call x6 -> x3, Pallas kernels: 432 us -> 408 us  [connected(): pl.pallas_call(kernel, out_shape=outs, in_specs=in_specs, out_specs=out_s...]
    slice x12 -> x1, local copies, waits for them, and re-layouts: 16.4 us -> 0.7 us  [local_split(): sum_up_bias = small_sums[5:9, :own].reshape(-1)]
    reduce_sum x9 -> x0, other arithmetic: 15.7 us -> none  [the longest x3 5.58 us: norm_parts(): centred = values - jnp.mean(values, axis=-1, keepdims=True)]
    unnamed x122 -> x17, local copies, waits for them, and re-layouts: 19.8 us -> 4.54 us
    another operation x4 -> x0, other arithmetic: 7.91 us -> none
where the time goes in v3:
time: 442 us; the launch traced here: 438 us
  Pallas kernels  408 us (92%)
  local copies, waits for them, and re-layouts  15.5 us (4%)
  other arithmetic  13.4 us (3%)
    pallas_call x3, Pallas kernels, connected(): pl.pallas_call(kernel, out_shape=outs, in_specs=in_specs, out_specs=out_s...  408 us

profile of v3, /device:TPU:0, one launch (start us, length us, event | category | flops | bytes accessed | tf_op | source)
XLA Modules:
  0.0 438.0 jit_solution(16794503684301418683)
XLA Ops:
  0.6 0.7 pad.24
  4.0 0.7 reshape.147
  5.5 0.7 fusion.2.mask
  6.2 0.8 fusion.1.comb
  7.0 1.9 fusion.3
  8.9 1.3 pad_maximum_fusion.1
  10.2 0.9 convert_element_type.78
  11.2 1.8 fusion.9
  13.5 1.9 pad_maximum_fusion.suffix
  15.4 182.3 %shard_map.245 = (bf16[4,256,1536]{2,1,0:T(8,128)(2,1)}, bf16[4,256,1536]{2,1,0:T(8,128)(2,1)}, bf16[4,256,1152]{2,1,0:T(8,128)(2,1)}, bf16[4,256,384]{2,1,0:T(8...) custom-call(bf16[256,1536]{1,0:T(8,128)(2,1)} %bitcast.49, ...), custom_call_target="tpu_custom_call" | custom-call | tf_op jit(solution)/shard_map/pallas_call | solution.py:1352
  197.6 57.0 %shard_map.246 = (f32[256,1536]{1,0:T(8,128)}, f32[8,1536]{1,0:T(8,128)}, bf16[1,4,192,1536]{3,2,1,0:T(8,128)(2,1)}, bf16[4,4,48,1536]{3,2,1,0:T(8,128)(2,1)}, bf16[2,4,256,1536]{3,2,1,0:T(8,128)(2,1)}) custom-call(bf16[4,256,1536]{2,1,0:T(8,128)(2,1)} %get-tuple-element.38.all_ffn_in, bf16[2,4,256,1536]{3,2,1,0:T(8,128)(2,1)} %get-tuple-element.39.incoming, ...), custom_call_target="tpu_custom_call" | custom-call | tf_op jit(solution)/shard_map/pallas_call | solution.py:1352
  254.6 2.4 convert_element_type.89.branch
  257.0 169.0 %shard_map.247 = (bf16[4,256,1536]{2,1,0:T(8,128)(2,1)}, bf16[256,1536]{1,0:T(8,128)(2,1)}, f32[192,1536]{1,0:T(8,128)}, f32[48,1536]{1,0:T(8,128)}, bf16[4,48,1...) custom-call(bf16[256,1536]{1,0:T(8,128)(2,1)} %convert_element_type.89.branch, ...), custom_call_target="tpu_custom_call" | custom-call | tf_op jit(solution)/shard_map/pallas_call | solution.py:1352
  426.0 0.7 slice.54
  426.7 1.4 slice_bitcast_fusion.3
  428.7 1.1 convert_bitcast_fusion.1
  429.9 0.7 copy.36
  430.7 0.7 copy.35
  431.4 0.7 copy.34
  432.3 1.1 copy.37
  433.6 1.7 copy.42
  435.2 0.9 copy.43
  436.1 0.7 copy.44
  436.8 1.0 copy.45
  (28 shorter events, 5.1 us)
Async XLA Ops:
  5.5 4.8 %copy-start.1 = (bf16[4,1,256,1536]{3,2,1,0:T(8,128)(2,1)S(1)}, bf16[4,1,256,1536]{3,2,1,0:T(8,128)(2,1)}, u32[]{:S(2)}) copy-start(bf16[4,1,256,1536]{3,2,1,0:T(8,128)(2,1)} %param.15) | copy-start | bytes 9437188
  428.7 3.4 copy-start.4
  431.4 2.2 copy-start
  433.6 1.7 copy-start.3
  433.6 2.6 copy-start.5
  435.2 1.6 copy-start.2
